TPU v7x, 256 devices: a whole 4x4x8 slice. The times are simulated.
256 devices in a mesh: row: 8 (over z_lo, core), col: 32 (over x, z_hi, y).
Axes of the slice: x: 4, y: 4, z: 8 (z_hi: 2, z_lo: 4; z = z_hi * 4 + z_lo), core: 2. Of those that a mesh axis runs over, the one named last changes fastest.
Arguments:
- weights: float32 [16384, 4, 4096], P('row', None, 'col'), may hold values from -6 to 6
- factor: float32 [4, 128, 4, 4096], P(None, 'row', None, 'col'), as said below
- keep_masks: int32 [128, 4, 128], P('row'), may hold values from 0 to 1, as said below
Outputs:
- pruned_weights: float32 [16384, 4, 4096], P('row', None, 'col')
Inputs may be any that keep to these rules, and one draw needn't show every extreme that they name: `keep_masks`: 1 keeps a weight; a group's mask of a block keeps exactly 64 of its columns, either two of every four consecutive columns or in no pattern. `factor`: zero where the column comes before the row; the diagonal entries lie between 0.5 and 2.
All inputs are finite; a program needn't handle non-finite values.
Results may differ from a plain program's by a relative error of at most 0.0001.
Values sent between devices are 32-bit elements; how exact they have to be, the bound alone decides.
No kernel may reach another device: no remote copies, remote signals or barrier semaphores. Data moves between devices by JAX's collectives and lax.ppermute only.
A program may use at most 64 MiB of HBM per device.

v0:
```python
import jax
import jax.numpy as jnp
from jax import lax
from jax.sharding import PartitionSpec as P


def broadcast(value, axis, source):
    kept = jnp.where(lax.axis_index(axis) == source, value, 0).astype(value.dtype)
    return lax.psum(kept, axis)


def unit_inverse(nilpotent, block_width):
    identity = jnp.eye(block_width, dtype=jnp.float32)
    inverse = identity[None, :, :] - nilpotent
    power = nilpotent
    span = 2
    while span < block_width:
        power = jnp.einsum("gik,gkj->gij", power, power, precision=lax.Precision.HIGHEST)
        inverse = jnp.einsum(
            "gik,gkj->gij", inverse, identity[None, :, :] + power, precision=lax.Precision.HIGHEST
        )
        span = span * 2
    return inverse


def solve_block(block_slab, triangle, keep_now):
    groups = keep_now.shape[0]
    block_width = triangle.shape[0]
    identity = jnp.eye(block_width, dtype=jnp.float32)
    pivots = jnp.sum(triangle * identity, axis=1)
    strict = jnp.triu(triangle, 1)
    keep_float = keep_now.astype(jnp.float32)
    scaling = (1.0 - keep_float) / pivots[None, :]
    nilpotent = strict[None, :, :] * scaling[:, None, :]
    inverse = unit_inverse(nilpotent, block_width)
    apply_map = scaling[:, :, None] * inverse
    grouped = block_slab.reshape(groups, -1, block_width)
    errors = jnp.einsum("grk,gkj->grj", grouped, apply_map, precision=lax.Precision.HIGHEST)
    current = grouped - jnp.einsum("grk,kj->grj", errors, strict, precision=lax.Precision.HIGHEST)
    kept_block = current * keep_float[:, None, :]
    return (errors.reshape(block_slab.shape), kept_block.reshape(block_slab.shape))


def fetch_factor(factor, block):
    piece = lax.dynamic_index_in_dim(factor, block, 0, keepdims=False)
    return lax.all_gather(piece, "row", axis=0, tiled=True)


def share_block(block_slab, triangle, keep_now, root_col):
    errors, kept_block = solve_block(block_slab, triangle, keep_now)
    errors = broadcast(errors, "col", root_col)
    return (errors, kept_block)


def store_block(pruned, kept_block, block, col_count):
    local_block = block // col_count
    is_owner = lax.axis_index("col") == block % col_count
    stored = lax.dynamic_index_in_dim(pruned, local_block, 1, keepdims=False)
    chosen = jnp.where(is_owner, kept_block, stored)
    return lax.dynamic_update_index_in_dim(pruned, chosen, local_block, 1)


def trailing(weights_now, errors, factor_block):
    return weights_now - jnp.einsum(
        "rk,kls->rls", errors, factor_block, precision=lax.Precision.HIGHEST
    )


def local(weights, factor, keep_masks):
    col_count = lax.axis_size("col")
    block_count = keep_masks.shape[1]
    pruned = jnp.zeros_like(weights)

    def block_step(block, loop_state):
        weights_now, pruned_now = loop_state
        factor_block = fetch_factor(factor, block)
        local_block = block // col_count
        block_slab = lax.dynamic_index_in_dim(weights_now, local_block, 1, keepdims=False)
        triangle = lax.dynamic_index_in_dim(factor_block, local_block, 1, keepdims=False)
        keep_now = lax.dynamic_index_in_dim(keep_masks, block, 1, keepdims=False)
        errors, kept_block = share_block(block_slab, triangle, keep_now, block % col_count)
        pruned_now = store_block(pruned_now, kept_block, block, col_count)
        return (trailing(weights_now, errors, factor_block), pruned_now)

    weights, pruned = lax.fori_loop(0, block_count, block_step, (weights, pruned))
    global_block = jnp.arange(weights.shape[1]) * col_count + lax.axis_index("col")
    pruned_cols = global_block < block_count
    return jnp.where(pruned_cols[None, :, None], pruned, weights)


def solution(mesh):
    placed = (P("row", None, "col"), P(None, "row", None, "col"), P("row", None, None))
    return jax.shard_map(
        local, mesh=mesh, in_specs=placed, out_specs=P("row", None, "col"), check_vma=False
    )
```

profile of v0, /device:TPU:198, one launch (start us, length us, event | category | flops | bytes accessed | tf_op | source)
XLA Modules:
  0.0 1887.6 jit_solution(10454172050461974999)
XLA Ops:
  6.5 4.4 copy.4
  10.9 2.3 broadcast_in_dim.59.clone
  13.2 1859.9 %while.17 = (s32[]{:T(128)}, f32[2048,4,128]{2,0,1:T(8,128)}, f32[2048,4,128]{2,1,0:T(4,128)}, s32[16,4,128]{2,1,0:T(4,128)}, f32[4,16,4,128]{3,2,1,0:T(4,128)},...) while((s32[]{:T(128)}, f32[2048,4,128]{2,0,1:T(8,128)}, ...), condition=%wide.region_3.4_spmd, body=%wide.region_0.3_spmd.sunk | while | flops 7252867072 | bytes 63440752 | solution.py:85
  14.0 13.3 all-gather.2
  41.1 1.3 constant_dynamic-slice_fusion.8
  43.6 2.2 broadcast_select_fusion.2
  45.8 2.7 constant_dynamic-slice_fusion.11
  49.7 27.6 %dynamic_update_slice.12 = f32[2048,4,128]{2,1,0:T(4,128)} dynamic-update-slice(f32[2048,4,128]{2,1,0:T(4,128)} %get-tuple-element.217, f32[2048,1,128]{2,1,0:T(1,128)S(1)} %bitcast.114, s32[]{:T(128)} %constant.155.clone.1..sunk, s32[]{:T(128)S(6)} %select_n.149, s32[]{:T(128)} %constant.155.clone.1..sunk) | dynamic-update-slice | bytes 2097156 | tf_op jit(solution)/shard_map/while/body/eval_jaxpr/jit(dynamic_update_index_in_dim)/dynamic_update_slice | solution.py:60
  77.2 384.0 %all-reduce.2.cloned.1.call-done = f32[2048,128]{1,0:T(8,128)} async-done(((f32[2048,128]{1,0:T(8,128)}), f32[2048,128]{1,0:T(8,128)}) %all-reduce.2.cloned.1.call-update) | async-done | bytes 1048592 | tf_op jit(solution)/shard_map/while/body/eval_jaxpr/psum | solution.py:9
  461.2 6.8 convolution_subtract_fusion.3
  468.8 13.7 all-gather.2
  496.2 1.3 constant_dynamic-slice_fusion.8
  498.7 2.2 broadcast_select_fusion.2
  500.9 2.7 constant_dynamic-slice_fusion.11
  504.8 27.6 %dynamic_update_slice.12 = f32[2048,4,128]{2,1,0:T(4,128)} dynamic-update-slice(f32[2048,4,128]{2,1,0:T(4,128)} %get-tuple-element.217, f32[2048,1,128]{2,1,0:T(1,128)S(1)} %bitcast.114, s32[]{:T(128)} %constant.155.clone.1..sunk, s32[]{:T(128)S(6)} %select_n.149, s32[]{:T(128)} %constant.155.clone.1..sunk) | dynamic-update-slice | bytes 2097156 | tf_op jit(solution)/shard_map/while/body/eval_jaxpr/jit(dynamic_update_index_in_dim)/dynamic_update_slice | solution.py:60
  532.3 397.3 %all-reduce.2.cloned.1.call-done = f32[2048,128]{1,0:T(8,128)} async-done(((f32[2048,128]{1,0:T(8,128)}), f32[2048,128]{1,0:T(8,128)}) %all-reduce.2.cloned.1.call-update) | async-done | bytes 1048592 | tf_op jit(solution)/shard_map/while/body/eval_jaxpr/psum | solution.py:9
  929.6 6.8 convolution_subtract_fusion.3
  937.1 13.7 all-gather.2
  964.5 1.3 constant_dynamic-slice_fusion.8
  967.1 2.2 broadcast_select_fusion.2
  969.3 2.7 constant_dynamic-slice_fusion.11
  973.1 27.6 %dynamic_update_slice.12 = f32[2048,4,128]{2,1,0:T(4,128)} dynamic-update-slice(f32[2048,4,128]{2,1,0:T(4,128)} %get-tuple-element.217, f32[2048,1,128]{2,1,0:T(1,128)S(1)} %bitcast.114, s32[]{:T(128)} %constant.155.clone.1..sunk, s32[]{:T(128)S(6)} %select_n.149, s32[]{:T(128)} %constant.155.clone.1..sunk) | dynamic-update-slice | bytes 2097156 | tf_op jit(solution)/shard_map/while/body/eval_jaxpr/jit(dynamic_update_index_in_dim)/dynamic_update_slice | solution.py:60
  1000.7 397.3 %all-reduce.2.cloned.1.call-done = f32[2048,128]{1,0:T(8,128)} async-done(((f32[2048,128]{1,0:T(8,128)}), f32[2048,128]{1,0:T(8,128)}) %all-reduce.2.cloned.1.call-update) | async-done | bytes 1048592 | tf_op jit(solution)/shard_map/while/body/eval_jaxpr/psum | solution.py:9
  1398.0 6.8 convolution_subtract_fusion.3
  1405.5 13.7 all-gather.2
  1432.9 1.3 constant_dynamic-slice_fusion.8
  1435.5 2.2 broadcast_select_fusion.2
  1437.7 2.7 constant_dynamic-slice_fusion.11
  1441.5 27.6 %dynamic_update_slice.12 = f32[2048,4,128]{2,1,0:T(4,128)} dynamic-update-slice(f32[2048,4,128]{2,1,0:T(4,128)} %get-tuple-element.217, f32[2048,1,128]{2,1,0:T(1,128)S(1)} %bitcast.114, s32[]{:T(128)} %constant.155.clone.1..sunk, s32[]{:T(128)S(6)} %select_n.149, s32[]{:T(128)} %constant.155.clone.1..sunk) | dynamic-update-slice | bytes 2097156 | tf_op jit(solution)/shard_map/while/body/eval_jaxpr/jit(dynamic_update_index_in_dim)/dynamic_update_slice | solution.py:60
  1469.1 397.3 %all-reduce.2.cloned.1.call-done = f32[2048,128]{1,0:T(8,128)} async-done(((f32[2048,128]{1,0:T(8,128)}), f32[2048,128]{1,0:T(8,128)}) %all-reduce.2.cloned.1.call-update) | async-done | bytes 1048592 | tf_op jit(solution)/shard_map/while/body/eval_jaxpr/psum | solution.py:9
  1866.4 6.8 convolution_subtract_fusion.3
  1873.1 7.9 copy_select_fusion
  (97 shorter events, 67.0 us)
Async XLA Ops:
  13.2 448.0 %all-reduce.2.cloned.1.call-start = ((), (), s32[]{:S(2)}) async-start(), calls=%async_computation | async-start | bytes 2097152 | tf_op jit(solution)/shard_map/while/body/eval_jaxpr/psum | solution.py:9
  468.0 461.6 %all-reduce.2.cloned.1.call-start = ((), (), s32[]{:S(2)}) async-start(), calls=%async_computation | async-start | bytes 2097152 | tf_op jit(solution)/shard_map/while/body/eval_jaxpr/psum | solution.py:9
  936.3 461.6 %all-reduce.2.cloned.1.call-start = ((), (), s32[]{:S(2)}) async-start(), calls=%async_computation | async-start | bytes 2097152 | tf_op jit(solution)/shard_map/while/body/eval_jaxpr/psum | solution.py:9
  1404.7 461.6 %all-reduce.2.cloned.1.call-start = ((), (), s32[]{:S(2)}) async-start(), calls=%async_computation | async-start | bytes 2097152 | tf_op jit(solution)/shard_map/while/body/eval_jaxpr/psum | solution.py:9
Sparse Core Ops, SparseCore 0:
  46.0 415.1 all-reduce.1
  501.1 428.4 all-reduce.1
  969.4 428.4 all-reduce.1
  1437.8 428.4 all-reduce.1
where the time goes:
time: 1910 us; the launch traced here: 1890 us
  waiting for transfers between devices  1580 us (83%)
  local copies, waits for them, and re-layouts  139 us (7%)
  matrix products  95.6 us (5%)
  blocking collectives  54.3 us (3%)
    psum x4, waiting for transfers between devices, broadcast(): return lax.psum(kept, axis)  1580 us
    dynamic_update_slice x4, local copies, waits for them, and re-layouts, store_block(): return lax.dynamic_update_index_in_dim(pruned, chosen, local_block, 1)  110 us
    all_gather x4, blocking collectives, fetch_factor(): return lax.all_gather(piece, 'row', axis=0, tiled=True)  54.3 us
  transfers between devices with their start and end apart: 4, of which 4 were waited for; matrix products, arithmetic and copies ran while one was open for 7% of the time, Pallas kernels for 0%

commit v1 on v0

v1 whole, which is shorter than its diff:
```python
import functools

import jax
import jax.numpy as jnp
from jax import lax
from jax.experimental import pallas as pl
from jax.experimental.pallas import tpu as pltpu
from jax.sharding import PartitionSpec as P

NX, NZ, NY, NZL = 4, 2, 4, 4
BW = 128
NB = 4
ACT = 64
KACT = NB * ACT
F32, BF16 = jnp.float32, jnp.bfloat16
NN = (((1,), (0,)), ((), ()))
NT = (((1,), (1,)), ((), ()))


def permute(value, move):
    pairs = []
    for row in range(2 * NZL):
        for x in range(NX):
            for z in range(NZ):
                for y in range(NY):
                    target = move(row >> 1, row & 1, x, z, y)
                    if target is not None:
                        zl, core, tx, tz, ty = target
                        pairs.append((device(row >> 1, row & 1, x, z, y), device(zl, core, tx, tz, ty)))
    return lax.ppermute(value, ("row", "col"), pairs)


def device(zl, core, x, z, y):
    return (zl * 2 + core) * (NX * NZ * NY) + (x * NZ + z) * NY + y


def shift(value, dx, dy):
    return permute(value, lambda zl, c, x, z, y: (zl, c, (x + dx) % NX, z, (y + dy) % NY))


def from_first_x(value, dx):
    return permute(value, lambda zl, c, x, z, y: (zl, c, dx, z, y) if x == 0 else None)


def to_second_plane(value):
    return permute(value, lambda zl, c, x, z, y: (zl, c, x, 1, y) if z == 0 else None)


def swap_core(value):
    return permute(value, lambda zl, c, x, z, y: (zl, 1 - c, x, z, y))


def swap_chip(value, j):
    return permute(value, lambda zl, c, x, z, y: (zl ^ j, c, x, z, y))


def owner_chips(value, j, plane):
    return permute(value, lambda zl, c, x, z, y: (zl ^ j, c, 0, plane, y) if x == 0 and z == 0 else None)


def dot(a, b, dims=NN):
    return lax.dot_general(a, b, dims, preferred_element_type=F32)


def split(value):
    high = value.astype(BF16)
    return high, (value - high.astype(F32)).astype(BF16)


def dot3(a, b):
    ah, al = split(a)
    bh, bl = split(b)
    return dot(ah, bh) + (dot(ah, bl) + dot(al, bh))


def compact_kernel(place_ref, w_ref, target_ref, out_ref):
    block = place_ref[0]
    rows = lax.broadcasted_iota(jnp.int32, (ACT, BW), 0) + block * ACT
    for group in range(target_ref.shape[0]):
        pick = (rows == target_ref[group, pl.ds(block, 1), :]).astype(F32).astype(BF16)
        slab = w_ref[pl.ds(group * BW * 4, BW, stride=4), :]
        high, rest = split(slab)
        mid, low = split(slab - high.astype(F32))
        out_ref[group] = dot(pick, high, NT) + (dot(pick, mid, NT) + dot(pick, low, NT))


def solve_kernel(place_ref, *refs):
    mine, others = refs[0:NY], refs[NY : 2 * NY]
    w_ref, target_ref, out_ref, tri_ref, slab_ref = refs[2 * NY :]
    y, group, zl, core = place_ref[0], place_ref[1], place_ref[2], place_ref[3]
    inner = BW // (2 * NZL)
    for s in range(NY):
        block = (y + (NY - s)) & (NY - 1)
        for q, piece in ((0, mine[s]), (1, others[s])):
            for j in range(NZL):
                owner = ((zl ^ j) * 2 + (core ^ q)) * inner
                for b in range(NB):
                    tri_ref[block, pl.ds(pl.multiple_of(b * BW + owner, inner), inner), :] = piece[
                        (j * NB + b) * inner : (j * NB + b + 1) * inner, :
                    ]
        slab_ref[pl.ds(pl.multiple_of(block * ACT, ACT), ACT), :] = w_ref[s]
    rows = lax.broadcasted_iota(jnp.int32, (KACT, BW), 0)
    pick = jnp.concatenate(
        [(rows == target_ref[group, b : b + 1, :]).astype(F32).astype(BF16) for b in range(NB)], axis=1
    )
    full = jnp.concatenate([tri_ref[b] for b in range(NB)], axis=1)
    high, low = split(full)
    high = dot(pick, high).astype(BF16)
    low = dot(pick, low).astype(BF16)
    active = dot(high, pick, NT) + dot(low, pick, NT)
    row_id = lax.broadcasted_iota(jnp.int32, (KACT, KACT), 0)
    col_ids = lax.broadcasted_iota(jnp.int32, (KACT, KACT), 1)
    diagonal = jnp.where(row_id == col_ids, active, 0.0)
    scale_down = 1.0 / jnp.sum(diagonal, axis=1, keepdims=True)
    scale_across = 1.0 / jnp.sum(diagonal, axis=0, keepdims=True)
    strict = jnp.where(row_id < col_ids, active, 0.0) * scale_down
    differ = row_id ^ col_ids
    inverse = jnp.where(row_id == col_ids, 1.0, 0.0) - jnp.where(differ == 1, strict, 0.0)
    size = 2
    while size < KACT:
        cross = jnp.where((differ >= size) & (differ < 2 * size), strict, 0.0)
        inverse = inverse - dot3(inverse, dot3(cross, inverse))
        size *= 2
    slab = slab_ref[...].T
    out_ref[...] = dot3(slab, inverse) * scale_across


def layout_kernel(place_ref, *refs):
    mine, others = refs[0:NZL], refs[NZL]
    high_ref, low_ref = refs[NZL + 1 :]
    zl, core = place_ref[0], place_ref[1]
    inner = BW // (2 * NZL)
    for j in range(NZL):
        for q in range(2):
            owner = ((zl ^ j) * 2 + (core ^ q)) * inner
            for b in range(NB):
                for l in range(4):
                    rows = pl.ds(b * inner * 4 + l, inner, stride=4)
                    value = mine[j][rows, :] if q == 0 else others[j, rows, :]
                    high, low = split(value)
                    here = (pl.ds(pl.multiple_of(b * BW + owner, inner), inner), slice(l * BW, (l + 1) * BW))
                    high_ref[here] = high
                    low_ref[here] = low


def update_kernel(place_ref, groups_ref, w_ref, high_ref, low_ref, target_ref, *refs, pieces, first):
    errors = refs[: len(pieces[0])]
    refs = refs[len(pieces[0]) :]
    out_ref, buf_ref, pick_ref, ed_high, ed_low, upd_ref, in_sem, out_sem = refs[0 if first else 1 :]
    y, owner = place_ref[0], place_ref[1]
    half = BW // 2
    plan = pieces[1]
    size = 4 * BW

    def rows_of(k):
        return pl.ds(pl.multiple_of(groups_ref[k] * size, size), size)

    count = len(plan)
    for k in range(count):
        pltpu.make_async_copy(w_ref.at[rows_of(k)], buf_ref.at[k], in_sem.at[k]).start()
    pick_ref[...] = jnp.zeros_like(pick_ref)
    rows = lax.broadcasted_iota(jnp.int32, (ACT, BW), 0)
    start = 0
    while start < count:
        many = min(3, count - start)
        for k in range(start, start + many):
            group = groups_ref[k]
            for b in range(NB):
                pick = (rows + b * ACT == target_ref[group, b : b + 1, :]).astype(F32).astype(BF16)
                pick_ref[b * ACT : (b + 1) * ACT, b * BW : (b + 1) * BW] = pick
            pick = pick_ref[...]
            here = slice((k - start) * BW, (k - start + 1) * BW)
            what = plan[k]
            if len(what) == 1:
                value = errors[what[0]][...]
            else:
                (r0, i0), (r1, i1) = what
                value = jnp.concatenate([errors[r0][i0], errors[r1][i1]], axis=0)
            high, low = split(value)
            ed_high[here, :] = dot(high, pick).astype(BF16)
            ed_low[here, :] = dot(low, pick).astype(BF16)
        span = slice(0, many * BW)
        upd_ref[span, :] = dot(ed_high[span, :], high_ref[...]) + (
            dot(ed_high[span, :], low_ref[...]) + dot(ed_low[span, :], high_ref[...])
        )
        for k in range(start, start + many):
            group = groups_ref[k]
            pltpu.make_async_copy(w_ref.at[rows_of(k)], buf_ref.at[k], in_sem.at[k]).wait()
            kept = (target_ref[group, pl.ds(y, 1), :] < 0) | (owner == 0)
            for l in range(4):
                here = pl.ds(l, BW, stride=4)
                value = buf_ref[k, here, :] - upd_ref[(k - start) * BW : (k - start + 1) * BW, l * BW : (l + 1) * BW]
                if l == 0:
                    value = jnp.where(kept, value, 0.0)
                buf_ref[k, here, :] = value
            pltpu.make_async_copy(buf_ref.at[k], out_ref.at[rows_of(k)], out_sem.at[k]).start()
        start += many
    for k in range(count):
        pltpu.make_async_copy(buf_ref.at[k], out_ref.at[rows_of(k)], out_sem.at[k]).wait()


def whole(shape):
    return pl.BlockSpec(shape, lambda *_: (0,) * len(shape))


SMEM = pl.BlockSpec(memory_space=pltpu.SMEM)


ANY = pl.BlockSpec(memory_space=pl.ANY)


def scalars(*values):
    return jnp.stack(values).astype(jnp.int32)


def update(place, groups, flat, high, low, target, errors, plan, earlier=None):
    count = len(plan)
    first = earlier is None
    operands = [place, groups, flat, high, low, target, *errors] + ([] if first else [earlier])
    specs = [SMEM, SMEM, ANY] + [whole(v.shape) for v in operands[3 : 6 + len(errors)]] + ([] if first else [ANY])
    return pl.pallas_call(
        functools.partial(update_kernel, pieces=(errors, plan), first=first),
        out_shape=jax.ShapeDtypeStruct(flat.shape, F32),
        in_specs=specs,
        out_specs=ANY,
        input_output_aliases={} if first else {len(operands) - 1: 0},
        scratch_shapes=[
            pltpu.VMEM((count, 4 * BW, BW), F32),
            pltpu.VMEM((KACT, NB * BW), BF16),
            pltpu.VMEM((3 * BW, NB * BW), BF16),
            pltpu.VMEM((3 * BW, NB * BW), BF16),
            pltpu.VMEM((3 * BW, 4 * BW), F32),
            pltpu.SemaphoreType.DMA((count,)),
            pltpu.SemaphoreType.DMA((count,)),
        ],
        compiler_params=pltpu.CompilerParams(vmem_limit_bytes=40 << 20),
        cost_estimate=pl.CostEstimate(flops=count * 2**28, bytes_accessed=count * 2**19, transcendentals=0),
    )(*operands)


def local(weights, factor, keep_masks):
    me, row = lax.axis_index("col"), lax.axis_index("row")
    x, z, y = me >> 3, (me >> 2) & 1, me & 3
    zl, core = row >> 1, row & 1
    groups = keep_masks.shape[0]
    rows = weights.shape[0]
    flat = weights.reshape(rows * 4, BW)
    barrier = lax.optimization_barrier

    with jax.named_scope("triangle_rows"):
        mine = factor[:, :, 0, :].reshape(-1, BW)
        near = [owner_chips(mine, j, 0) for j in range(1, NZL)]
        far = [owner_chips(mine, j, 1) for j in range(NZL)]

    with jax.named_scope("compact"):
        pruned = 1 - keep_masks
        before = jnp.triu(jnp.ones((BW, BW), BF16), 1)
        rank = lax.dot_general(
            pruned.astype(BF16), before, (((2,), (0,)), ((), ())), preferred_element_type=F32
        ).astype(jnp.int32)
        target = jnp.where(pruned == 1, rank + ACT * jnp.arange(NB, dtype=jnp.int32)[None, :, None], -1)
        compact = pl.pallas_call(
            compact_kernel,
            out_shape=jax.ShapeDtypeStruct((groups, ACT, BW), F32),
            in_specs=[SMEM, whole(flat.shape), whole((groups, NB, BW))],
            out_specs=whole((groups, ACT, BW)),
            grid=(1,),
            compiler_params=pltpu.CompilerParams(vmem_limit_bytes=40 << 20),
            cost_estimate=pl.CostEstimate(flops=2**30, bytes_accessed=2**24, transcendentals=0),
        )(scalars(y), flat, target)

    with jax.named_scope("triangle_x"):
        tri = jnp.stack(
            [jnp.where(z == 1, far[0], mine)] + [near[j - 1] + far[j] for j in range(1, NZL)]
        ).reshape(-1, BW)
        tri, compact = barrier((tri, compact))
        moved = [from_first_x(tri, dx) for dx in (1, 2, 3)]

    with jax.named_scope("slab_y"):
        pieces = [lax.dynamic_slice_in_dim(compact, y * NX, NX, 0)]
        for s in (1, 2, 3):
            piece = lax.dynamic_slice_in_dim(compact, ((y + s) & 3) * NX, NX, 0)
            pieces.append(shift(piece, 0, s))

    with jax.named_scope("factor_chips"):
        tri, moved, factor = barrier((tri, moved, factor))
        here = factor.reshape(-1, BW)
        chips = [here] + [swap_chip(here, j) for j in range(1, NZL)]

    with jax.named_scope("triangle_y"):
        tri = jnp.where(x == 0, tri, moved[0] + moved[1] + moved[2])
        tris = [tri] + [shift(tri, 0, s) for s in (1, 2, 3)]

    with jax.named_scope("slab_x"):
        stacked = jnp.stack(pieces, axis=1)
        moved = [from_first_x(stacked[dx], dx) for dx in (1, 2, 3)]
        slab = jnp.where(x == 0, stacked[0], moved[0] + moved[1] + moved[2])

    with jax.named_scope("slab_z"):
        slab = jnp.where(z == 1, to_second_plane(slab), slab)

    with jax.named_scope("triangle_core"):
        others = [swap_core(piece) for piece in tris]

    with jax.named_scope("factor_core"):
        other_chips = swap_core(jnp.stack(chips))

    with jax.named_scope("solve"):
        errors = pl.pallas_call(
            solve_kernel,
            out_shape=jax.ShapeDtypeStruct((BW, KACT), F32),
            in_specs=[SMEM] + [whole((NB * BW // 2, BW))] * 8 + [whole((NB, ACT, BW)), whole((groups, NB, BW))],
            out_specs=whole((BW, KACT)),
            grid=(1,),
            scratch_shapes=[pltpu.VMEM((NB, NB * BW, BW), F32), pltpu.VMEM((KACT, BW), F32)],
            compiler_params=pltpu.CompilerParams(vmem_limit_bytes=32 << 20),
            cost_estimate=pl.CostEstimate(flops=2**31, bytes_accessed=2**21, transcendentals=0),
        )(scalars(y, y * NX + x, zl, core), *tris, *others, slab, target)

    with jax.named_scope("layout"):
        high, low = pl.pallas_call(
            layout_kernel,
            out_shape=[jax.ShapeDtypeStruct((NB * BW, 4 * BW), BF16)] * 2,
            in_specs=[SMEM] + [whole((4 * BW // 2, BW))] * 4 + [whole((4, 4 * BW // 2, BW))],
            out_specs=[whole((NB * BW, 4 * BW))] * 2,
            grid=(1,),
            cost_estimate=pl.CostEstimate(flops=2**20, bytes_accessed=2**22, transcendentals=0),
        )(scalars(zl, core), *chips, other_chips)

    with jax.named_scope("errors_near"):
        half = BW // 2
        by_y = [shift(errors, 0, s) for s in (1, 2, 3)]
        by_x = [shift(errors, t, 0) for t in (1, 2, 3)]
        by_x, by_y, high, low = barrier((by_x, by_y, high, low))

    with jax.named_scope("errors_far"):
        top = jnp.stack([piece[:half] for piece in by_y])
        bottom = jnp.stack([piece[half:] for piece in by_x])
        top_x = [shift(top, t, 0) for t in (1, 2, 3)]
        bottom_y = [shift(bottom, 0, s) for s in (1, 2, 3)]

    with jax.named_scope("update"):
        place = scalars(y, ((x == 0) & (z == 0)).astype(jnp.int32))

        def group_of(s, t):
            return ((y + (NY - s)) & 3) * NX + ((x + (NX - t)) & 3)

        first = [(0, 0)] + [(s, 0) for s in (1, 2, 3)] + [(0, t) for t in (1, 2, 3)]
        out = update(
            place, scalars(*[group_of(*p) for p in first]), flat, high, low, target,
            [errors, *by_y, *by_x], [(k,) for k in range(7)],
        )
        out, top_x, bottom_y = barrier((out, top_x, bottom_y))
        second = [(s, t) for s in (1, 2, 3) for t in (1, 2, 3)]
        out = update(
            place, scalars(*[group_of(*p) for p in second]), flat, high, low, target,
            [*top_x, *bottom_y], [((t - 1, s - 1), (3 + s - 1, t - 1)) for s, t in second], out,
        )
    return out.reshape(weights.shape)


def solution(mesh):
    placed = (P("row", None, "col"), P(None, "row", None, "col"), P("row", None, None))
    return jax.shard_map(
        local, mesh=mesh, in_specs=placed, out_specs=P("row", None, "col"), check_vma=False
    )
```

time: 1910 us -> 125 us (0.07)
  the two profiles are of different devices: /device:TPU:198 before, /device:TPU:30 now
where the time goes in v1:
time: 125 us; the launch traced here: 124 us
  starting transfers between devices  54.5 us (44%)
  waiting for transfers between devices  39.3 us (31%)
  Pallas kernels  19.5 us (16%)
  local copies, waits for them, and re-layouts  7.69 us (6%)
  other arithmetic  2.57 us (2%)
    ppermute x40, starting transfers between devices, permute(): return lax.ppermute(value, ('row', 'col'), pairs)  54.5 us
    ppermute x40, waiting for transfers between devices, permute(): return lax.ppermute(value, ('row', 'col'), pairs)  39.3 us
    pallas_call x2, Pallas kernels, update(): pl.pallas_call(functools.partial(update_kernel, pieces=(errors, plan), fi...  9.61 us
    unnamed x18, local copies, waits for them, and re-layouts  6.48 us
    pallas_call x1, Pallas kernels, local(): pl.pallas_call(solve_kernel, out_shape=jax.ShapeDtypeStruct((BW, KACT), F...  6.21 us
  transfers between devices with their start and end apart: 40, of which 11 were waited for; matrix products, arithmetic and copies ran while one was open for 2% of the time, Pallas kernels for 11%

profile of v1, /device:TPU:30, one launch (start us, length us, event | category | flops | bytes accessed | tf_op | source)
XLA Modules:
  0.0 124.3 jit_solution(5412076775193513656)
XLA Ops:
  6.0 2.2 %copy-done = f32[2048,4,128]{2,1,0:T(4,128)S(1)} copy-done((f32[2048,4,128]{2,1,0:T(4,128)S(1)}, f32[2048,4,128]{2,1,0:T(4,128)}, u32[]{:S(2)}) %copy-start) | copy-done | bytes 4194328
  8.2 1.2 compact.1
  10.9 1.3 %collective-permute-start.9 = (f32[256,128]{1,0:T(8,128)S(1)}, f32[256,128]{1,0:T(8,128)S(1)}, u32[]{:S(2)}, u32[]{:S(2)}) collective-permute-start(f32[256,128]{1,0:T(8,128)S(1)} %bitcast.76), channel_id=1, source_target_pairs={{0,24},{1,25},{2,26},{3,27},{4,28},{5,29},{6,30},{7,31},{32,56},{3... | collective-permute-start | bytes 393224 | tf_op jit(solution)/shard_map/triangle_x/ppermute | solution.py:30
  15.4 19.2 %collective-permute-done.9 = f32[256,128]{1,0:T(8,128)S(1)} collective-permute-done((f32[256,128]{1,0:T(8,128)S(1)}, f32[256,128]{1,0:T(8,128)S(1)}, u32[]{:S(2)}, u32[]{:S(2)}) %collective-permute-start.9) | collective-permute-done | bytes 131104 | tf_op jit(solution)/shard_map/triangle_x/ppermute | solution.py:30
  34.8 4.7 %collective-permute-done.17 = f32[4,64,128]{2,1,0:T(8,128)S(1)} collective-permute-done((f32[4,64,128]{2,1,0:T(8,128)S(1)}, f32[4,64,128]{2,1,0:T(8,128)S(1)}, u32[]{:S(2)}, u32[]{:S(2)}) %collective-permute-start.17) | collective-permute-done | bytes 131104 | tf_op jit(solution)/shard_map/slab_y/ppermute | solution.py:30
  40.3 1.3 %collective-permute-start.22 = (f32[4,64,128]{2,1,0:T(8,128)S(1)}, f32[4,64,128]{2,1,0:T(8,128)S(1)}, u32[]{:S(2)}, u32[]{:S(2)}) collective-permute-start(f32[4,64,128]{2,1,0:T(8,128)S(1)} %get-tuple-element.54), channel_id=1, source_target_pairs={{0,24},{1,25},{2,26},{3,27},{4,28},{5,29},{6,30},{7,31},{32,56},{3... | collective-permute-start | bytes 393224 | tf_op jit(solution)/shard_map/slab_x/ppermute | solution.py:30
  43.1 2.2 %collective-permute-start.11 = (f32[256,128]{1,0:T(8,128)S(1)}, f32[256,128]{1,0:T(8,128)S(1)}, u32[]{:S(2)}, u32[]{:S(2)}) collective-permute-start(f32[256,128]{1,0:T(8,128)S(1)} %add_select_fusion.refs_0_), channel_id=1, source_target_pairs={{0,2},{1,3},{2,0},{3,1},{4,6},{5,7},{6,4},{7,5},{8,10},{9,11},{10,... | collective-permute-start | bytes 393224 | tf_op jit(solution)/shard_map/triangle_y/ppermute | solution.py:30
  45.2 1.9 %collective-permute-start.32 = (f32[256,128]{1,0:T(8,128)S(1)}, f32[256,128]{1,0:T(8,128)S(1)}, u32[]{:S(2)}, u32[]{:S(2)}) collective-permute-start(f32[256,128]{1,0:T(8,128)S(1)} %bitcast.72), channel_id=1, source_target_pairs={{0,192},{1,193},{2,194},{3,195},{4,196},{5,197},{6,198},{7,199},{8... | collective-permute-start | bytes 393224 | tf_op jit(solution)/shard_map/factor_chips/ppermute | solution.py:30
  47.2 1.3 %collective-permute-done.22 = f32[4,64,128]{2,1,0:T(8,128)S(1)} collective-permute-done((f32[4,64,128]{2,1,0:T(8,128)S(1)}, f32[4,64,128]{2,1,0:T(8,128)S(1)}, u32[]{:S(2)}, u32[]{:S(2)}) %collective-permute-start.22) | collective-permute-done | bytes 131104 | tf_op jit(solution)/shard_map/slab_x/ppermute | solution.py:30
  48.4 1.1 collective-permute-start.31
  50.6 1.9 %collective-permute-done.32.refs_3_ = f32[256,128]{1,0:T(8,128)S(1)} collective-permute-done((f32[256,128]{1,0:T(8,128)S(1)}, f32[256,128]{1,0:T(8,128)S(1)}, u32[]{:S(2)}, u32[]{:S(2)}) %collective-permute-start.32) | collective-permute-done | bytes 131104 | tf_op jit(solution)/shard_map/factor_chips/ppermute | solution.py:30
  52.5 1.9 %collective-permute-start.10 = (f32[256,128]{1,0:T(8,128)S(1)}, f32[256,128]{1,0:T(8,128)S(1)}, u32[]{:S(2)}, u32[]{:S(2)}) collective-permute-start(f32[256,128]{1,0:T(8,128)S(1)} %add_select_fusion.refs_0_), channel_id=1, source_target_pairs={{0,1},{1,2},{2,3},{3,0},{4,5},{5,6},{6,7},{7,4},{8,9},{9,10},{10,1... | collective-permute-start | bytes 393224 | tf_op jit(solution)/shard_map/triangle_y/ppermute | solution.py:30
  54.4 1.7 %collective-permute-done.31.refs_2_ = f32[256,128]{1,0:T(8,128)S(1)} collective-permute-done((f32[256,128]{1,0:T(8,128)S(1)}, f32[256,128]{1,0:T(8,128)S(1)}, u32[]{:S(2)}, u32[]{:S(2)}) %collective-permute-start.31) | collective-permute-done | bytes 131104 | tf_op jit(solution)/shard_map/factor_chips/ppermute | solution.py:30
  56.1 7.9 %collective-permute-start.23 = (f32[4,64,128]{2,1,0:T(8,128)S(1)}, f32[4,64,128]{2,1,0:T(8,128)S(1)}, u32[]{:S(2)}, u32[]{:S(2)}) collective-permute-start(f32[4,64,128]{2,1,0:T(8,128)S(1)} %fusion), channel_id=1, source_target_pairs={{0,4},{1,5},{2,6},{3,7},{8,12},{9,13},{10,14},{11,15},{16,20},{17,... | collective-permute-start | bytes 393224 | tf_op jit(solution)/shard_map/slab_z/ppermute | solution.py:30
  65.4 1.2 collective-permute-done.23
  66.8 1.1 collective-permute-done.14.refs_5_
  67.9 6.2 %solve.1.refs_0_ = f32[128,256]{1,0:T(8,128)S(1)} custom-call(s32[4]{0:T(128)S(1)} %pad_add_fusion.1.place_ref, f32[256,128]{1,0:T(8,128)S(1)} %add_select_fusion.refs_0_, f32[256,128]{1,0:T(8,128)S(1)} %collective-permute-done.10.refs_1_, f32[256,128]{1,0:T(8,128)S(1)} %collective-permute-done.11.refs_2_, f32[256,128]{1,0:T(8,128)S(1)} %collective-permute-done.12.refs_3_, ...), custom_call_target="tpu_custom_call" | custom-call | flops 2147483648 | bytes 2097152 | tf_op jit(solution)/shard_map/solve/pallas_call | solution.py:309
  74.8 3.3 %collective-permute-start.28 = (f32[128,256]{1,0:T(8,128)S(1)}, f32[128,256]{1,0:T(8,128)S(1)}, u32[]{:S(2)}, u32[]{:S(2)}) collective-permute-start(f32[128,256]{1,0:T(8,128)S(1)} %solve.1.refs_0_), channel_id=1, source_target_pairs={{0,2},{1,3},{2,0},{3,1},{4,6},{5,7},{6,4},{7,5},{8,10},{9,11},{10,... | collective-permute-start | bytes 393224 | tf_op jit(solution)/shard_map/errors_near/ppermute | solution.py:30
  78.1 1.9 %collective-permute-start.26 = (f32[128,256]{1,0:T(8,128)S(1)}, f32[128,256]{1,0:T(8,128)S(1)}, u32[]{:S(2)}, u32[]{:S(2)}) collective-permute-start(f32[128,256]{1,0:T(8,128)S(1)} %solve.1.refs_0_), channel_id=1, source_target_pairs={{0,24},{1,25},{2,26},{3,27},{4,28},{5,29},{6,30},{7,31},{8,0},{9,1... | collective-permute-start | bytes 393224 | tf_op jit(solution)/shard_map/errors_near/ppermute | solution.py:30
  80.0 1.2 collective-permute-done.29.refs_3_
  81.2 2.7 %collective-permute-start.25 = (f32[128,256]{1,0:T(8,128)S(1)}, f32[128,256]{1,0:T(8,128)S(1)}, u32[]{:S(2)}, u32[]{:S(2)}) collective-permute-start(f32[128,256]{1,0:T(8,128)S(1)} %solve.1.refs_0_), channel_id=1, source_target_pairs={{0,16},{1,17},{2,18},{3,19},{4,20},{5,21},{6,22},{7,23},{8,24},{9,... | collective-permute-start | bytes 393224 | tf_op jit(solution)/shard_map/errors_near/ppermute | solution.py:30
  83.9 4.9 %collective-permute-start.24 = (f32[128,256]{1,0:T(8,128)S(1)}, f32[128,256]{1,0:T(8,128)S(1)}, u32[]{:S(2)}, u32[]{:S(2)}) collective-permute-start(f32[128,256]{1,0:T(8,128)S(1)} %solve.1.refs_0_), channel_id=1, source_target_pairs={{0,8},{1,9},{2,10},{3,11},{4,12},{5,13},{6,14},{7,15},{8,16},{9,17... | collective-permute-start | bytes 393224 | tf_op jit(solution)/shard_map/errors_near/ppermute | solution.py:30
  89.4 2.5 %layout.1 = (bf16[512,512]{1,0:T(8,128)(2,1)}, bf16[512,512]{1,0:T(8,128)(2,1)}) custom-call(s32[2]{0:T(128)} %pad_add_fusion.2.place_ref, f32[256,128]{1,0:T(8,128)} %bitcast.71, f32[256,128]{1,0:T(8,128)} %copy-done.8, f32[256,128]{1,0:T(8,128)} %copy-done.7, f32[256,128]{1,0:T(8,128)} %copy-done.6, f32[4,256,128]{2,1,0:T(8,128)} %copy-done.5), custom_call_target="tpu_custom_call" | custom-call | flops 1048576 | bytes 4194304 | tf_op jit(solution)/shard_map/layout/pallas_call | solution.py:321
  92.0 3.4 %collective-permute-done.24.refs_4_ = f32[128,256]{1,0:T(8,128)S(1)} collective-permute-done((f32[128,256]{1,0:T(8,128)S(1)}, f32[128,256]{1,0:T(8,128)S(1)}, u32[]{:S(2)}, u32[]{:S(2)}) %collective-permute-start.24) | collective-permute-done | bytes 131104 | tf_op jit(solution)/shard_map/errors_near/ppermute | solution.py:30
  96.3 2.4 %collective-permute-start.37 = (f32[3,64,256]{2,1,0:T(8,128)S(1)}, f32[3,64,256]{2,1,0:T(8,128)S(1)}, u32[]{:S(2)}, u32[]{:S(2)}) collective-permute-start(f32[3,64,256]{2,1,0:T(8,128)S(1)} %pad_maximum_fusion.3), channel_id=1, source_target_pairs={{0,1},{1,2},{2,3},{3,0},{4,5},{5,6},{6,7},{7,4},{8,9},{9,10},{10,1... | collective-permute-start | bytes 589832 | tf_op jit(solution)/shard_map/errors_far/ppermute | solution.py:30
  99.1 3.6 %collective-permute-start.35 = (f32[3,64,256]{2,1,0:T(8,128)S(1)}, f32[3,64,256]{2,1,0:T(8,128)S(1)}, u32[]{:S(2)}, u32[]{:S(2)}) collective-permute-start(f32[3,64,256]{2,1,0:T(8,128)S(1)} %pad_maximum_fusion.2), channel_id=1, source_target_pairs={{0,16},{1,17},{2,18},{3,19},{4,20},{5,21},{6,22},{7,23},{8,24},{9,... | collective-permute-start | bytes 589832 | tf_op jit(solution)/shard_map/errors_far/ppermute | solution.py:30
  102.7 3.4 %collective-permute-done.39.refs_5_ = f32[3,64,256]{2,1,0:T(8,128)S(1)} collective-permute-done((f32[3,64,256]{2,1,0:T(8,128)S(1)}, f32[3,64,256]{2,1,0:T(8,128)S(1)}, u32[]{:S(2)}, u32[]{:S(2)}) %collective-permute-start.39) | collective-permute-done | bytes 196640 | tf_op jit(solution)/shard_map/errors_far/ppermute | solution.py:30
  106.1 3.8 %collective-permute-start.34 = (f32[3,64,256]{2,1,0:T(8,128)S(1)}, f32[3,64,256]{2,1,0:T(8,128)S(1)}, u32[]{:S(2)}, u32[]{:S(2)}) collective-permute-start(f32[3,64,256]{2,1,0:T(8,128)S(1)} %pad_maximum_fusion.2), channel_id=1, source_target_pairs={{0,8},{1,9},{2,10},{3,11},{4,12},{5,13},{6,14},{7,15},{8,16},{9,17... | collective-permute-start | bytes 589832 | tf_op jit(solution)/shard_map/errors_far/ppermute | solution.py:30
  110.2 2.2 %copy-done.1 = f32[2048,4,128]{2,1,0:T(4,128)S(1)} copy-done((f32[2048,4,128]{2,1,0:T(4,128)S(1)}, f32[2048,4,128]{2,1,0:T(4,128)}, u32[]{:S(2)}) %copy-start.1) | copy-done | bytes 4194328
  112.4 1.0 copy-done.2
  114.5 4.4 %update.2.refs_6_ = f32[8192,128]{1,0:T(8,128)} custom-call(s32[2]{0:T(128)S(1)} %pad_add_fusion.place_ref, s32[7]{0:T(128)S(1)} %stack.191.groups_ref, f32[8192,128]{1,0:T(8,128)S(1)} %bitcast.69, bf16[512,512]{1,0:T(8,128)(2,1)S(1)} %copy-done.2, bf16[512,512]{1,0:T(8,128)(2,1)S(1)} %copy-done.3, s32[16,4,128]{2,1,0:T(4,128)S(1)} %fusion.6.target_ref.refs_9_, ...), custom_call_target="tpu_custom_call" | custom-call | flops 1879048192 | bytes 3670016 | tf_op jit(solution)/shard_map/update/pallas_call | solution.py:221
  118.9 5.2 %update.3 = f32[8192,128]{1,0:T(8,128)} custom-call(s32[2]{0:T(128)S(1)} %pad_add_fusion.place_ref, s32[9]{0:T(128)S(1)} %stack.164.groups_ref, f32[8192,128]{1,0:T(8,128)S(1)} %bitcast.70, bf16[512,512]{1,0:T(8,128)(2,1)S(1)} %copy-done.2, bf16[512,512]{1,0:T(8,128)(2,1)S(1)} %copy-done.3, ...), custom_call_target="tpu_custom_call", output_to_operand_aliasing={{}: (12, {})} | custom-call | flops 2415919104 | bytes 4718592 | tf_op jit(solution)/shard_map/update/pallas_call | solution.py:221
  (99 shorter events, 19.5 us)
Async XLA Ops:
  0.9 8.5 %collective-permute-start.6 = (f32[64,128]{1,0:T(8,128)S(1)}, f32[64,128]{1,0:T(8,128)S(1)}, u32[]{:S(2)}, u32[]{:S(2)}) collective-permute-start(f32[64,128]{1,0:T(8,128)S(1)} %bitcast.83), channel_id=1, source_target_pairs={{0,196},{1,197},{2,198},{3,199},{32,228},{33,229},{34,230},{35,231... | collective-permute-start | bytes 98312 | tf_op jit(solution)/shard_map/triangle_rows/ppermute | solution.py:30
  1.6 8.5 %collective-permute-start.5 = (f32[64,128]{1,0:T(8,128)S(1)}, f32[64,128]{1,0:T(8,128)S(1)}, u32[]{:S(2)}, u32[]{:S(2)}) collective-permute-start(f32[64,128]{1,0:T(8,128)S(1)} %bitcast.84), channel_id=1, source_target_pairs={{0,192},{1,193},{2,194},{3,195},{32,224},{33,225},{34,226},{35,227... | collective-permute-start | bytes 98312 | tf_op jit(solution)/shard_map/triangle_rows/ppermute | solution.py:30
  2.3 8.5 %collective-permute-start.4 = (f32[64,128]{1,0:T(8,128)S(1)}, f32[64,128]{1,0:T(8,128)S(1)}, u32[]{:S(2)}, u32[]{:S(2)}) collective-permute-start(f32[64,128]{1,0:T(8,128)S(1)} %bitcast.85), channel_id=1, source_target_pairs={{0,132},{1,133},{2,134},{3,135},{32,164},{33,165},{34,166},{35,167... | collective-permute-start | bytes 98312 | tf_op jit(solution)/shard_map/triangle_rows/ppermute | solution.py:30
  2.9 7.8 %collective-permute-start.3 = (f32[64,128]{1,0:T(8,128)S(1)}, f32[64,128]{1,0:T(8,128)S(1)}, u32[]{:S(2)}, u32[]{:S(2)}) collective-permute-start(f32[64,128]{1,0:T(8,128)S(1)} %bitcast.86), channel_id=1, source_target_pairs={{0,128},{1,129},{2,130},{3,131},{32,160},{33,161},{34,162},{35,163... | collective-permute-start | bytes 98312 | tf_op jit(solution)/shard_map/triangle_rows/ppermute | solution.py:30
  3.6 7.2 %collective-permute-start.2 = (f32[64,128]{1,0:T(8,128)S(1)}, f32[64,128]{1,0:T(8,128)S(1)}, u32[]{:S(2)}, u32[]{:S(2)}) collective-permute-start(f32[64,128]{1,0:T(8,128)S(1)} %bitcast.87), channel_id=1, source_target_pairs={{0,68},{1,69},{2,70},{3,71},{32,100},{33,101},{34,102},{35,103},{6... | collective-permute-start | bytes 98312 | tf_op jit(solution)/shard_map/triangle_rows/ppermute | solution.py:30
  10.9 23.6 %collective-permute-start.9 = (f32[256,128]{1,0:T(8,128)S(1)}, f32[256,128]{1,0:T(8,128)S(1)}, u32[]{:S(2)}, u32[]{:S(2)}) collective-permute-start(f32[256,128]{1,0:T(8,128)S(1)} %bitcast.76), channel_id=1, source_target_pairs={{0,24},{1,25},{2,26},{3,27},{4,28},{5,29},{6,30},{7,31},{32,56},{3... | collective-permute-start | bytes 393224 | tf_op jit(solution)/shard_map/triangle_x/ppermute | solution.py:30
  12.2 22.6 %collective-permute-start.8 = (f32[256,128]{1,0:T(8,128)S(1)}, f32[256,128]{1,0:T(8,128)S(1)}, u32[]{:S(2)}, u32[]{:S(2)}) collective-permute-start(f32[256,128]{1,0:T(8,128)S(1)} %bitcast.77), channel_id=1, source_target_pairs={{0,16},{1,17},{2,18},{3,19},{4,20},{5,21},{6,22},{7,23},{32,48},{3... | collective-permute-start | bytes 393224 | tf_op jit(solution)/shard_map/triangle_x/ppermute | solution.py:30
  12.9 21.9 %collective-permute-start.7 = (f32[256,128]{1,0:T(8,128)S(1)}, f32[256,128]{1,0:T(8,128)S(1)}, u32[]{:S(2)}, u32[]{:S(2)}) collective-permute-start(f32[256,128]{1,0:T(8,128)S(1)} %bitcast.78), channel_id=1, source_target_pairs={{0,8},{1,9},{2,10},{3,11},{4,12},{5,13},{6,14},{7,15},{32,40},{33,... | collective-permute-start | bytes 393224 | tf_op jit(solution)/shard_map/triangle_x/ppermute | solution.py:30
  13.6 21.1 %collective-permute-start.19 = (f32[4,64,128]{2,1,0:T(8,128)S(1)}, f32[4,64,128]{2,1,0:T(8,128)S(1)}, u32[]{:S(2)}, u32[]{:S(2)}) collective-permute-start(f32[4,64,128]{2,1,0:T(8,128)S(1)} %get-tuple-element.57), channel_id=1, source_target_pairs={{0,3},{1,0},{2,1},{3,2},{4,7},{5,4},{6,5},{7,6},{8,11},{9,8},{10,9... | collective-permute-start | bytes 393224 | tf_op jit(solution)/shard_map/slab_y/ppermute | solution.py:30
  14.4 20.3 %collective-permute-start.18 = (f32[4,64,128]{2,1,0:T(8,128)S(1)}, f32[4,64,128]{2,1,0:T(8,128)S(1)}, u32[]{:S(2)}, u32[]{:S(2)}) collective-permute-start(f32[4,64,128]{2,1,0:T(8,128)S(1)} %get-tuple-element.58), channel_id=1, source_target_pairs={{0,2},{1,3},{2,0},{3,1},{4,6},{5,7},{6,4},{7,5},{8,10},{9,11},{10,... | collective-permute-start | bytes 393224 | tf_op jit(solution)/shard_map/slab_y/ppermute | solution.py:30
  40.3 8.2 %collective-permute-start.22 = (f32[4,64,128]{2,1,0:T(8,128)S(1)}, f32[4,64,128]{2,1,0:T(8,128)S(1)}, u32[]{:S(2)}, u32[]{:S(2)}) collective-permute-start(f32[4,64,128]{2,1,0:T(8,128)S(1)} %get-tuple-element.54), channel_id=1, source_target_pairs={{0,24},{1,25},{2,26},{3,27},{4,28},{5,29},{6,30},{7,31},{32,56},{3... | collective-permute-start | bytes 393224 | tf_op jit(solution)/shard_map/slab_x/ppermute | solution.py:30
  41.6 8.0 %collective-permute-start.20 = (f32[4,64,128]{2,1,0:T(8,128)S(1)}, f32[4,64,128]{2,1,0:T(8,128)S(1)}, u32[]{:S(2)}, u32[]{:S(2)}) collective-permute-start(f32[4,64,128]{2,1,0:T(8,128)S(1)} %get-tuple-element.55), channel_id=1, source_target_pairs={{0,8},{1,9},{2,10},{3,11},{4,12},{5,13},{6,14},{7,15},{32,40},{33,... | collective-permute-start | bytes 393224 | tf_op jit(solution)/shard_map/slab_x/ppermute | solution.py:30
  42.3 22.0 %collective-permute-start.12 = (f32[256,128]{1,0:T(8,128)S(1)}, f32[256,128]{1,0:T(8,128)S(1)}, u32[]{:S(2)}, u32[]{:S(2)}) collective-permute-start(f32[256,128]{1,0:T(8,128)S(1)} %add_select_fusion.refs_0_), channel_id=1, source_target_pairs={{0,3},{1,0},{2,1},{3,2},{4,7},{5,4},{6,5},{7,6},{8,11},{9,8},{10,9... | collective-permute-start | bytes 393224 | tf_op jit(solution)/shard_map/triangle_y/ppermute | solution.py:30
  43.1 21.8 %collective-permute-start.11 = (f32[256,128]{1,0:T(8,128)S(1)}, f32[256,128]{1,0:T(8,128)S(1)}, u32[]{:S(2)}, u32[]{:S(2)}) collective-permute-start(f32[256,128]{1,0:T(8,128)S(1)} %add_select_fusion.refs_0_), channel_id=1, source_target_pairs={{0,2},{1,3},{2,0},{3,1},{4,6},{5,7},{6,4},{7,5},{8,10},{9,11},{10,... | collective-permute-start | bytes 393224 | tf_op jit(solution)/shard_map/triangle_y/ppermute | solution.py:30
  45.2 7.2 %collective-permute-start.32 = (f32[256,128]{1,0:T(8,128)S(1)}, f32[256,128]{1,0:T(8,128)S(1)}, u32[]{:S(2)}, u32[]{:S(2)}) collective-permute-start(f32[256,128]{1,0:T(8,128)S(1)} %bitcast.72), channel_id=1, source_target_pairs={{0,192},{1,193},{2,194},{3,195},{4,196},{5,197},{6,198},{7,199},{8... | collective-permute-start | bytes 393224 | tf_op jit(solution)/shard_map/factor_chips/ppermute | solution.py:30
  48.4 7.7 %collective-permute-start.31 = (f32[256,128]{1,0:T(8,128)S(1)}, f32[256,128]{1,0:T(8,128)S(1)}, u32[]{:S(2)}, u32[]{:S(2)}) collective-permute-start(f32[256,128]{1,0:T(8,128)S(1)} %bitcast.73), channel_id=1, source_target_pairs={{0,128},{1,129},{2,130},{3,131},{4,132},{5,133},{6,134},{7,135},{8... | collective-permute-start | bytes 393224 | tf_op jit(solution)/shard_map/factor_chips/ppermute | solution.py:30
  49.5 14.6 %collective-permute-start.30 = (f32[256,128]{1,0:T(8,128)S(1)}, f32[256,128]{1,0:T(8,128)S(1)}, u32[]{:S(2)}, u32[]{:S(2)}) collective-permute-start(f32[256,128]{1,0:T(8,128)S(1)} %bitcast.74), channel_id=1, source_target_pairs={{0,64},{1,65},{2,66},{3,67},{4,68},{5,69},{6,70},{7,71},{8,72},{9,... | collective-permute-start | bytes 393224 | tf_op jit(solution)/shard_map/factor_chips/ppermute | solution.py:30
  52.5 12.5 %collective-permute-start.10 = (f32[256,128]{1,0:T(8,128)S(1)}, f32[256,128]{1,0:T(8,128)S(1)}, u32[]{:S(2)}, u32[]{:S(2)}) collective-permute-start(f32[256,128]{1,0:T(8,128)S(1)} %add_select_fusion.refs_0_), channel_id=1, source_target_pairs={{0,1},{1,2},{2,3},{3,0},{4,5},{5,6},{6,7},{7,4},{8,9},{9,10},{10,1... | collective-permute-start | bytes 393224 | tf_op jit(solution)/shard_map/triangle_y/ppermute | solution.py:30
  56.1 10.4 %collective-permute-start.23 = (f32[4,64,128]{2,1,0:T(8,128)S(1)}, f32[4,64,128]{2,1,0:T(8,128)S(1)}, u32[]{:S(2)}, u32[]{:S(2)}) collective-permute-start(f32[4,64,128]{2,1,0:T(8,128)S(1)} %fusion), channel_id=1, source_target_pairs={{0,4},{1,5},{2,6},{3,7},{8,12},{9,13},{10,14},{11,15},{16,20},{17,... | collective-permute-start | bytes 393224 | tf_op jit(solution)/shard_map/slab_z/ppermute | solution.py:30
  64.3 19.6 %collective-permute-start.33 = (f32[4,256,128]{2,1,0:T(8,128)S(1)}, f32[4,256,128]{2,1,0:T(8,128)S(1)}, u32[]{:S(2)}, u32[]{:S(2)}) collective-permute-start(f32[4,256,128]{2,1,0:T(8,128)S(1)} %pad_maximum_fusion.1), channel_id=1, source_target_pairs={{0,32},{1,33},{2,34},{3,35},{4,36},{5,37},{6,38},{7,39},{8,40},{9,... | collective-permute-start | bytes 1572872 | tf_op jit(solution)/shard_map/factor_core/ppermute | solution.py:30
  74.1 7.0 %collective-permute-start.29 = (f32[128,256]{1,0:T(8,128)S(1)}, f32[128,256]{1,0:T(8,128)S(1)}, u32[]{:S(2)}, u32[]{:S(2)}) collective-permute-start(f32[128,256]{1,0:T(8,128)S(1)} %solve.1.refs_0_), channel_id=1, source_target_pairs={{0,3},{1,0},{2,1},{3,2},{4,7},{5,4},{6,5},{7,6},{8,11},{9,8},{10,9... | collective-permute-start | bytes 393224 | tf_op jit(solution)/shard_map/errors_near/ppermute | solution.py:30
  74.8 17.1 %collective-permute-start.28 = (f32[128,256]{1,0:T(8,128)S(1)}, f32[128,256]{1,0:T(8,128)S(1)}, u32[]{:S(2)}, u32[]{:S(2)}) collective-permute-start(f32[128,256]{1,0:T(8,128)S(1)} %solve.1.refs_0_), channel_id=1, source_target_pairs={{0,2},{1,3},{2,0},{3,1},{4,6},{5,7},{6,4},{7,5},{8,10},{9,11},{10,... | collective-permute-start | bytes 393224 | tf_op jit(solution)/shard_map/errors_near/ppermute | solution.py:30
  78.1 13.9 %collective-permute-start.27 = (f32[128,256]{1,0:T(8,128)S(1)}, f32[128,256]{1,0:T(8,128)S(1)}, u32[]{:S(2)}, u32[]{:S(2)}) collective-permute-start(f32[128,256]{1,0:T(8,128)S(1)} %solve.1.refs_0_), channel_id=1, source_target_pairs={{0,1},{1,2},{2,3},{3,0},{4,5},{5,6},{6,7},{7,4},{8,9},{9,10},{10,1... | collective-permute-start | bytes 393224 | tf_op jit(solution)/shard_map/errors_near/ppermute | solution.py:30
  78.1 13.8 %collective-permute-start.26 = (f32[128,256]{1,0:T(8,128)S(1)}, f32[128,256]{1,0:T(8,128)S(1)}, u32[]{:S(2)}, u32[]{:S(2)}) collective-permute-start(f32[128,256]{1,0:T(8,128)S(1)} %solve.1.refs_0_), channel_id=1, source_target_pairs={{0,24},{1,25},{2,26},{3,27},{4,28},{5,29},{6,30},{7,31},{8,0},{9,1... | collective-permute-start | bytes 393224 | tf_op jit(solution)/shard_map/errors_near/ppermute | solution.py:30
  81.2 10.8 %collective-permute-start.25 = (f32[128,256]{1,0:T(8,128)S(1)}, f32[128,256]{1,0:T(8,128)S(1)}, u32[]{:S(2)}, u32[]{:S(2)}) collective-permute-start(f32[128,256]{1,0:T(8,128)S(1)} %solve.1.refs_0_), channel_id=1, source_target_pairs={{0,16},{1,17},{2,18},{3,19},{4,20},{5,21},{6,22},{7,23},{8,24},{9,... | collective-permute-start | bytes 393224 | tf_op jit(solution)/shard_map/errors_near/ppermute | solution.py:30
  83.9 11.5 %collective-permute-start.24 = (f32[128,256]{1,0:T(8,128)S(1)}, f32[128,256]{1,0:T(8,128)S(1)}, u32[]{:S(2)}, u32[]{:S(2)}) collective-permute-start(f32[128,256]{1,0:T(8,128)S(1)} %solve.1.refs_0_), channel_id=1, source_target_pairs={{0,8},{1,9},{2,10},{3,11},{4,12},{5,13},{6,14},{7,15},{8,16},{9,17... | collective-permute-start | bytes 393224 | tf_op jit(solution)/shard_map/errors_near/ppermute | solution.py:30
  95.4 10.7 %collective-permute-start.39 = (f32[3,64,256]{2,1,0:T(8,128)S(1)}, f32[3,64,256]{2,1,0:T(8,128)S(1)}, u32[]{:S(2)}, u32[]{:S(2)}) collective-permute-start(f32[3,64,256]{2,1,0:T(8,128)S(1)} %pad_maximum_fusion.3), channel_id=1, source_target_pairs={{0,3},{1,0},{2,1},{3,2},{4,7},{5,4},{6,5},{7,6},{8,11},{9,8},{10,9... | collective-permute-start | bytes 589832 | tf_op jit(solution)/shard_map/errors_far/ppermute | solution.py:30
  95.5 23.4 %collective-permute-start.38 = (f32[3,64,256]{2,1,0:T(8,128)S(1)}, f32[3,64,256]{2,1,0:T(8,128)S(1)}, u32[]{:S(2)}, u32[]{:S(2)}) collective-permute-start(f32[3,64,256]{2,1,0:T(8,128)S(1)} %pad_maximum_fusion.3), channel_id=1, source_target_pairs={{0,2},{1,3},{2,0},{3,1},{4,6},{5,7},{6,4},{7,5},{8,10},{9,11},{10,... | collective-permute-start | bytes 589832 | tf_op jit(solution)/shard_map/errors_far/ppermute | solution.py:30
  96.3 22.6 %collective-permute-start.37 = (f32[3,64,256]{2,1,0:T(8,128)S(1)}, f32[3,64,256]{2,1,0:T(8,128)S(1)}, u32[]{:S(2)}, u32[]{:S(2)}) collective-permute-start(f32[3,64,256]{2,1,0:T(8,128)S(1)} %pad_maximum_fusion.3), channel_id=1, source_target_pairs={{0,1},{1,2},{2,3},{3,0},{4,5},{5,6},{6,7},{7,4},{8,9},{9,10},{10,1... | collective-permute-start | bytes 589832 | tf_op jit(solution)/shard_map/errors_far/ppermute | solution.py:30
  98.8 20.1 %collective-permute-start.36 = (f32[3,64,256]{2,1,0:T(8,128)S(1)}, f32[3,64,256]{2,1,0:T(8,128)S(1)}, u32[]{:S(2)}, u32[]{:S(2)}) collective-permute-start(f32[3,64,256]{2,1,0:T(8,128)S(1)} %pad_maximum_fusion.2), channel_id=1, source_target_pairs={{0,24},{1,25},{2,26},{3,27},{4,28},{5,29},{6,30},{7,31},{8,0},{9,1... | collective-permute-start | bytes 589832 | tf_op jit(solution)/shard_map/errors_far/ppermute | solution.py:30
  99.1 19.8 %collective-permute-start.35 = (f32[3,64,256]{2,1,0:T(8,128)S(1)}, f32[3,64,256]{2,1,0:T(8,128)S(1)}, u32[]{:S(2)}, u32[]{:S(2)}) collective-permute-start(f32[3,64,256]{2,1,0:T(8,128)S(1)} %pad_maximum_fusion.2), channel_id=1, source_target_pairs={{0,16},{1,17},{2,18},{3,19},{4,20},{5,21},{6,22},{7,23},{8,24},{9,... | collective-permute-start | bytes 589832 | tf_op jit(solution)/shard_map/errors_far/ppermute | solution.py:30
  106.1 12.8 %collective-permute-start.34 = (f32[3,64,256]{2,1,0:T(8,128)S(1)}, f32[3,64,256]{2,1,0:T(8,128)S(1)}, u32[]{:S(2)}, u32[]{:S(2)}) collective-permute-start(f32[3,64,256]{2,1,0:T(8,128)S(1)} %pad_maximum_fusion.2), channel_id=1, source_target_pairs={{0,8},{1,9},{2,10},{3,11},{4,12},{5,13},{6,14},{7,15},{8,16},{9,17... | collective-permute-start | bytes 589832 | tf_op jit(solution)/shard_map/errors_far/ppermute | solution.py:30
  (17 other events, 118.8 us)

commit v2 on v1

v2 whole, which is shorter than its diff:
```python
import functools

import jax
import jax.numpy as jnp
from jax import lax
from jax.experimental import pallas as pl
from jax.experimental.pallas import tpu as pltpu
from jax.sharding import PartitionSpec as P

NX, NZ, NY, NZL = 4, 2, 4, 4
BW = 128
NB = 4
ACT = 64
KACT = NB * ACT
F32, BF16 = jnp.float32, jnp.bfloat16
NN = (((1,), (0,)), ((), ()))
NT = (((1,), (1,)), ((), ()))


def permute(value, move):
    pairs = []
    for row in range(2 * NZL):
        for x in range(NX):
            for z in range(NZ):
                for y in range(NY):
                    target = move(row >> 1, row & 1, x, z, y)
                    if target is not None:
                        zl, core, tx, tz, ty = target
                        pairs.append((device(row >> 1, row & 1, x, z, y), device(zl, core, tx, tz, ty)))
    return lax.ppermute(value, ("row", "col"), pairs)


def device(zl, core, x, z, y):
    return (zl * 2 + core) * (NX * NZ * NY) + (x * NZ + z) * NY + y


def shift(value, dx, dy, planes=(0, 1)):
    return permute(
        value, lambda zl, c, x, z, y: (zl, c, (x + dx) % NX, z, (y + dy) % NY) if z in planes else None
    )


def from_first_x(value, dx):
    return permute(value, lambda zl, c, x, z, y: (zl, c, dx, z, y) if x == 0 and z == 0 else None)


def to_second_plane(value):
    return permute(value, lambda zl, c, x, z, y: (zl, c, x, 1, y) if z == 0 else None)


def swap_core(value, planes=(0, 1)):
    return permute(value, lambda zl, c, x, z, y: (zl, 1 - c, x, z, y) if z in planes else None)


def swap_chip(value, j, owners=False):
    return permute(
        value,
        lambda zl, c, x, z, y: (zl ^ j, c, x, z, y) if not owners or (x == 0 and z == 0) else None,
    )


def dot(a, b, dims=NN):
    return lax.dot_general(a, b, dims, preferred_element_type=F32)


def split(value):
    high = value.astype(BF16)
    return high, (value - high.astype(F32)).astype(BF16)


def dot3(a, b):
    ah, al = split(a)
    bh, bl = split(b)
    return dot(jnp.concatenate([ah, ah, al], axis=1), jnp.concatenate([bh, bl, bh], axis=0))


def compact_kernel(place_ref, w_ref, target_ref, out_ref):
    block = place_ref[1]
    rows = lax.broadcasted_iota(jnp.int32, (ACT, BW), 0) + block * ACT
    for group in range(target_ref.shape[0]):
        pick = (rows == target_ref[group, pl.ds(block, 1), :]).astype(F32).astype(BF16)
        slab = w_ref[pl.ds(group * BW * 4, BW, stride=4), :]
        high, rest = split(slab)
        mid, low = split(slab - high.astype(F32))
        out_ref[group] = dot(pick, high, NT) + (dot(pick, mid, NT) + dot(pick, low, NT))


def solve_kernel(place_ref, *refs):
    mine, others, far = refs[0:NY], refs[NY], refs[NY + 1]
    w_ref, target_ref, out_ref, tri_ref, slab_ref = refs[NY + 2 :]
    x, y, zl, core = place_ref[0], place_ref[1], place_ref[2], place_ref[3]
    group = y * NX + x
    inner = BW // (2 * NZL)
    for s in range(NY):
        block = (y + (NY - s)) & (NY - 1)
        for q, piece in ((0, mine[s]), (1, others if s == 0 else far.at[s - 1])):
            for j in range(NZL):
                owner = ((zl ^ j) * 2 + (core ^ q)) * inner
                for b in range(NB):
                    tri_ref[block, pl.ds(pl.multiple_of(b * BW + owner, inner), inner), :] = piece[
                        (j * NB + b) * inner : (j * NB + b + 1) * inner, :
                    ]
        slab_ref[pl.ds(pl.multiple_of(block * ACT, ACT), ACT), :] = (
            w_ref[...] if s == 0 else mine[s][NB * BW // 2 :, :]
        )
    rows = lax.broadcasted_iota(jnp.int32, (KACT, BW), 0)
    pick = jnp.concatenate(
        [(rows == target_ref[group, b : b + 1, :]).astype(F32).astype(BF16) for b in range(NB)], axis=1
    )
    full = jnp.concatenate([tri_ref[b] for b in range(NB)], axis=1)
    high, low = split(full)
    high = dot(pick, high).astype(BF16)
    low = dot(pick, low).astype(BF16)
    active = dot(high, pick, NT) + dot(low, pick, NT)
    row_id = lax.broadcasted_iota(jnp.int32, (KACT, KACT), 0)
    col_ids = lax.broadcasted_iota(jnp.int32, (KACT, KACT), 1)
    diagonal = jnp.where(row_id == col_ids, active, 0.0)
    scale_down = 1.0 / jnp.sum(diagonal, axis=1, keepdims=True)
    scale_across = 1.0 / jnp.sum(diagonal, axis=0, keepdims=True)
    strict = jnp.where(row_id < col_ids, active, 0.0) * scale_down
    differ = row_id ^ col_ids
    inverse = jnp.where(row_id == col_ids, 1.0, 0.0) - jnp.where(differ == 1, strict, 0.0)
    size = 2
    while size < KACT:
        cross = jnp.where((differ >= size) & (differ < 2 * size), strict, 0.0)
        inverse = inverse - dot3(inverse, dot3(cross, inverse))
        size *= 2
    slab = slab_ref[...].T
    out_ref[...] = dot3(slab, inverse) * scale_across


def layout_kernel(place_ref, *refs):
    mine, others = refs[0:2], refs[2:4]
    out_ref = refs[4]
    zl, core = place_ref[2], place_ref[3]
    inner = BW // (2 * NZL)
    for j in range(NZL):
        for q in range(2):
            owner = ((zl ^ j) * 2 + (core ^ q)) * inner
            for b in range(NB):
                for l in range(4):
                    rows = pl.ds(b * inner * 4 + l, inner, stride=4)
                    value = (mine, others)[q][j // 2][j % 2, rows, :]
                    high, low = split(value)
                    for part, piece in enumerate((high, low, high)):
                        start = pl.multiple_of((part * NB + b) * BW + owner, inner)
                        out_ref[pl.ds(start, inner), l * BW : (l + 1) * BW] = piece


def update_kernel(place_ref, w_ref, spread_ref, target_ref, *refs, pieces, first):
    errors = refs[: len(pieces[0])]
    refs = refs[len(pieces[0]) :]
    out_ref, buf_ref, pick_ref, ed_ref, upd_ref, in_sem, out_sem = refs[0 if first else 1 :]
    x, y, owner = place_ref[0], place_ref[1], place_ref[4]
    plan, places = pieces[1], pieces[2]
    which = [((y + (NY - s)) & 3) * NX + ((x + (NX - t)) & 3) for s, t in places]
    size = 4 * BW

    def rows_of(k):
        return pl.ds(pl.multiple_of(which[k] * size, size), size)

    count = len(plan)
    for k in range(count):
        pltpu.make_async_copy(w_ref.at[rows_of(k)], buf_ref.at[k], in_sem.at[k]).start()
    pick_ref[...] = jnp.zeros_like(pick_ref)
    rows = lax.broadcasted_iota(jnp.int32, (ACT, BW), 0)
    start = 0
    while start < count:
        many = min(3, count - start)
        for k in range(start, start + many):
            group = which[k]
            for b in range(NB):
                pick = (rows + b * ACT == target_ref[group, b : b + 1, :]).astype(F32).astype(BF16)
                pick_ref[b * ACT : (b + 1) * ACT, b * BW : (b + 1) * BW] = pick
            pick = pick_ref[...]
            here = slice((k - start) * BW, (k - start + 1) * BW)
            what = plan[k]
            if len(what) == 1:
                value = errors[what[0]][...]
            else:
                (r0, i0), (r1, i1) = what
                value = jnp.concatenate([errors[r0][i0], errors[r1][i1]], axis=0)
            high, low = split(value)
            wide = NB * BW
            high = dot(high, pick).astype(BF16)
            ed_ref[here, 0:wide] = high
            ed_ref[here, wide : 2 * wide] = high
            ed_ref[here, 2 * wide :] = dot(low, pick).astype(BF16)
        span = slice(0, many * BW)
        upd_ref[span, :] = dot(ed_ref[span, :], spread_ref[...])
        for k in range(start, start + many):
            group = which[k]
            pltpu.make_async_copy(w_ref.at[rows_of(k)], buf_ref.at[k], in_sem.at[k]).wait()
            kept = (target_ref[group, pl.ds(y, 1), :] < 0) | (owner == 0)
            for l in range(4):
                here = pl.ds(l, BW, stride=4)
                value = buf_ref[k, here, :] - upd_ref[(k - start) * BW : (k - start + 1) * BW, l * BW : (l + 1) * BW]
                if l == 0:
                    value = jnp.where(kept, value, 0.0)
                buf_ref[k, here, :] = value
            pltpu.make_async_copy(buf_ref.at[k], out_ref.at[rows_of(k)], out_sem.at[k]).start()
        start += many
    for k in range(count):
        pltpu.make_async_copy(buf_ref.at[k], out_ref.at[rows_of(k)], out_sem.at[k]).wait()


def whole(shape):
    return pl.BlockSpec(shape, lambda *_: (0,) * len(shape))


SMEM = pl.BlockSpec(memory_space=pltpu.SMEM)


ANY = pl.BlockSpec(memory_space=pl.ANY)


def scalars(*values):
    return jnp.stack([jnp.asarray(v, jnp.int32) for v in values])


def update(place, flat, spread, target, errors, plan, places, earlier=None):
    count = len(plan)
    first = earlier is None
    operands = [place, flat, spread, target, *errors] + ([] if first else [earlier])
    specs = [SMEM, ANY] + [whole(v.shape) for v in operands[2 : 4 + len(errors)]] + ([] if first else [ANY])
    return pl.pallas_call(
        functools.partial(update_kernel, pieces=(errors, plan, places), first=first),
        out_shape=jax.ShapeDtypeStruct(flat.shape, F32),
        in_specs=specs,
        out_specs=ANY,
        input_output_aliases={} if first else {len(operands) - 1: 0},
        scratch_shapes=[
            pltpu.VMEM((count, 4 * BW, BW), F32),
            pltpu.VMEM((KACT, NB * BW), BF16),
            pltpu.VMEM((3 * BW, 3 * NB * BW), BF16),
            pltpu.VMEM((3 * BW, 4 * BW), F32),
            pltpu.SemaphoreType.DMA((count,)),
            pltpu.SemaphoreType.DMA((count,)),
        ],
        compiler_params=pltpu.CompilerParams(vmem_limit_bytes=50 << 20),
        cost_estimate=pl.CostEstimate(flops=count * 2**28, bytes_accessed=count * 2**19, transcendentals=0),
    )(*operands)


def local(weights, factor, keep_masks):
    me, row = lax.axis_index("col"), lax.axis_index("row")
    x, z, y = me >> 3, (me >> 2) & 1, me & 3
    zl, core = row >> 1, row & 1
    groups = keep_masks.shape[0]
    rows = weights.shape[0]
    flat = weights.reshape(rows * 4, BW)
    barrier = lax.optimization_barrier
    place = scalars(x, y, zl, core, (x == 0) & (z == 0))

    with jax.named_scope("triangle_rows"):
        here = factor.reshape(-1, BW)
        near = swap_chip(here, 1)

    with jax.named_scope("compact"):
        pruned = 1 - keep_masks
        before = jnp.triu(jnp.ones((BW, BW), BF16), 1)
        rank = lax.dot_general(
            pruned.astype(BF16), before, (((2,), (0,)), ((), ())), preferred_element_type=F32
        ).astype(jnp.int32)
        target = jnp.where(pruned == 1, rank + ACT * jnp.arange(NB, dtype=jnp.int32)[None, :, None], -1)
        compact = pl.pallas_call(
            compact_kernel,
            out_shape=jax.ShapeDtypeStruct((groups, ACT, BW), F32),
            in_specs=[SMEM, whole(flat.shape), whole((groups, NB, BW))],
            out_specs=whole((groups, ACT, BW)),
            grid=(1,),
            compiler_params=pltpu.CompilerParams(vmem_limit_bytes=40 << 20),
            cost_estimate=pl.CostEstimate(flops=2**30, bytes_accessed=2**24, transcendentals=0),
        )(place, flat, target)

    with jax.named_scope("triangle_pairs"):
        near, compact = barrier((near, compact))
        chips = [jnp.stack([here, near])]
        pair = chips[0].reshape(2, -1, 4, BW)[:, :, 0, :]
        pair_far = swap_chip(pair, 2, True)

    with jax.named_scope("slab_x"):
        by_owner = compact.reshape(NY, NX, ACT, BW)
        moved = [from_first_x(by_owner[:, dx], dx) for dx in (1, 2, 3)]
        slabs = jnp.where(x == 0, by_owner[:, 0], moved[0] + moved[1] + moved[2])

    with jax.named_scope("triangle_x"):
        tri = jnp.concatenate([pair, pair_far]).reshape(-1, BW)
        tri, chips = barrier((tri, chips))
        moved = [from_first_x(tri, dx) for dx in (1, 2, 3)]

    with jax.named_scope("factor_chips"):
        chips = [chips[0], swap_chip(chips[0], 2)]

    with jax.named_scope("triangle_y"):
        tri = jnp.where(x == 0, tri, moved[0] + moved[1] + moved[2])
        mixed = []
        for s in (1, 2, 3):
            piece = lax.dynamic_index_in_dim(slabs, (y + s) & 3, 0, keepdims=False)
            mixed.append(shift(jnp.concatenate([tri, piece]), 0, s, (0,)))
        slab = lax.dynamic_index_in_dim(slabs, y, 0, keepdims=False)

    with jax.named_scope("triangle_core"):
        tri, mixed, chips = barrier((tri, mixed, chips))
        others = swap_core(jnp.stack([piece[: NB * BW // 2] for piece in mixed]), (0,))
        other = swap_core(tri, (0,))

    with jax.named_scope("factor_core"):
        other_chips = [swap_core(piece) for piece in chips]

    with jax.named_scope("solve"):
        errors = pl.pallas_call(
            solve_kernel,
            out_shape=jax.ShapeDtypeStruct((BW, KACT), F32),
            in_specs=[SMEM, whole(tri.shape)] + [whole(mixed[0].shape)] * 3
            + [whole(v.shape) for v in (other, others, slab, target)],
            out_specs=whole((BW, KACT)),
            grid=(1,),
            scratch_shapes=[pltpu.VMEM((NB, NB * BW, BW), F32), pltpu.VMEM((KACT, BW), F32)],
            compiler_params=pltpu.CompilerParams(vmem_limit_bytes=32 << 20),
            cost_estimate=pl.CostEstimate(flops=2**31, bytes_accessed=2**21, transcendentals=0),
        )(place, tri, *mixed, other, others, slab, target)

    with jax.named_scope("errors_plane"):
        errors, other_chips = barrier((errors, other_chips))
        errors = jnp.where(z == 1, to_second_plane(errors), errors)

    with jax.named_scope("errors_near"):
        half = BW // 2
        by_y = [shift(errors, 0, s) for s in (1, 2, 3)]
        by_x = [shift(errors, t, 0) for t in (1, 2, 3)]

    with jax.named_scope("layout"):
        spread = pl.pallas_call(
            layout_kernel,
            out_shape=jax.ShapeDtypeStruct((3 * NB * BW, 4 * BW), BF16),
            in_specs=[SMEM] + [whole((2, 4 * BW // 2, BW))] * 4,
            out_specs=whole((3 * NB * BW, 4 * BW)),
            grid=(1,),
            compiler_params=pltpu.CompilerParams(vmem_limit_bytes=16 << 20),
            cost_estimate=pl.CostEstimate(flops=2**28, bytes_accessed=2**23, transcendentals=0),
        )(place, *chips, *other_chips)

    with jax.named_scope("errors_far"):
        top = jnp.stack([piece[:half] for piece in by_y])
        bottom = jnp.stack([piece[half:] for piece in by_x])
        top_x = [shift(top, t, 0) for t in (1, 2, 3)]
        bottom_y = [shift(bottom, 0, s) for s in (1, 2, 3)]

    with jax.named_scope("update"):
        first = [(0, 0)] + [(s, 0) for s in (1, 2, 3)] + [(0, t) for t in (1, 2, 3)]
        out = update(
            place, flat, spread, target,
            [errors, *by_y, *by_x], [(k,) for k in range(7)], first,
        )
        out, top_x, bottom_y = barrier((out, top_x, bottom_y))
        second = [(s, t) for s in (1, 2, 3) for t in (1, 2, 3)]
        out = update(
            place, flat, spread, target,
            [*top_x, *bottom_y], [((t - 1, s - 1), (3 + s - 1, t - 1)) for s, t in second], second, out,
        )
    return out.reshape(weights.shape)


def solution(mesh):
    placed = (P("row", None, "col"), P(None, "row", None, "col"), P("row", None, None))
    return jax.shard_map(
        local, mesh=mesh, in_specs=placed, out_specs=P("row", None, "col"), check_vma=False
    )
```

time: 125 us -> 99.8 us (0.80)
  the two profiles are of different devices: /device:TPU:30 before, /device:TPU:198 now
where the time goes in v2:
time: 99.8 us; the launch traced here: 99.2 us
  waiting for transfers between devices  48.6 us (49%)
  starting transfers between devices  27.7 us (28%)
  Pallas kernels  18 us (18%)
  local copies, waits for them, and re-layouts  2.4 us (2%)
  other arithmetic  1.88 us (2%)
    ppermute x29, waiting for transfers between devices, permute(): return lax.ppermute(value, ('row', 'col'), pairs)  48.6 us
    ppermute x29, starting transfers between devices, permute(): return lax.ppermute(value, ('row', 'col'), pairs)  27.7 us
    pallas_call x2, Pallas kernels, update(): pl.pallas_call(functools.partial(update_kernel, pieces=(errors, plan, pla...  9.33 us
    pallas_call x1, Pallas kernels, local(): pl.pallas_call(solve_kernel, out_shape=jax.ShapeDtypeStruct((BW, KACT), F...  6.21 us
    unnamed x4, local copies, waits for them, and re-layouts  2.21 us
  transfers between devices with their start and end apart: 29, of which 6 were waited for; matrix products, arithmetic and copies ran while one was open for 2% of the time, Pallas kernels for 13%

profile of v2, /device:TPU:198, one launch (start us, length us, event | category | flops | bytes accessed | tf_op | source)
XLA Modules:
  0.0 99.2 jit_solution(8801974516091731300)
XLA Ops:
  0.0 1.0 %collective-permute-start = (f32[256,128]{1,0:T(8,128)}, f32[256,128]{1,0:T(8,128)S(1)}, u32[]{:S(2)}, u32[]{:S(2)}) collective-permute-start(f32[256,128]{1,0:T(8,128)} %bitcast.67), channel_id=1, source_target_pairs={{0,64},{1,65},{2,66},{3,67},{4,68},{5,69},{6,70},{7,71},{8,72},{9,... | collective-permute-start | bytes 393224 | tf_op jit(solution)/shard_map/triangle_rows/ppermute | solution.py:30
  1.0 0.8 subtract_convert_fusion
  1.9 0.8 fusion.6.target_ref.refs_7_
  2.9 2.2 %copy-done = f32[2048,4,128]{2,1,0:T(4,128)S(1)} copy-done((f32[2048,4,128]{2,1,0:T(4,128)S(1)}, f32[2048,4,128]{2,1,0:T(4,128)}, u32[]{:S(2)}) %copy-start) | copy-done | bytes 4194328
  5.0 1.7 %compact.1 = f32[16,64,128]{2,1,0:T(8,128)S(1)} custom-call(s32[5]{0:T(128)S(1)} %stack.75.place_ref, f32[8192,128]{1,0:T(8,128)S(1)} %bitcast.64, s32[16,4,128]{2,1,0:T(4,128)S(1)} %fusion.6.target_ref.refs_7_), custom_call_target="tpu_custom_call" | custom-call | flops 1073741824 | bytes 16777216 | tf_op jit(solution)/shard_map/compact/pallas_call | solution.py:266
  7.5 0.7 collective-permute-start.6
  8.2 0.7 collective-permute-start.5
  8.9 0.7 collective-permute-start.7
  11.7 1.5 %collective-permute-start.11 = (f32[2,256,128]{2,1,0:T(8,128)S(1)}, f32[2,256,128]{2,1,0:T(8,128)S(1)}, u32[]{:S(2)}, u32[]{:S(2)}) collective-permute-start(f32[2,256,128]{2,1,0:T(8,128)S(1)} %pad_maximum_fusion.1.refs_0_), channel_id=1, source_target_pairs={{0,128},{1,129},{2,130},{3,131},{4,132},{5,133},{6,134},{7,135},{8... | collective-permute-start | bytes 786440 | tf_op jit(solution)/shard_map/factor_chips/ppermute | solution.py:30
  13.4 0.7 collective-permute-start.10
  14.1 0.7 collective-permute-start.9
  14.8 0.7 collective-permute-start.8
  15.4 8.7 %collective-permute-done.11.refs_1_ = f32[2,256,128]{2,1,0:T(8,128)S(1)} collective-permute-done((f32[2,256,128]{2,1,0:T(8,128)S(1)}, f32[2,256,128]{2,1,0:T(8,128)S(1)}, u32[]{:S(2)}, u32[]{:S(2)}) %collective-permute-start.11) | collective-permute-done | bytes 262176 | tf_op jit(solution)/shard_map/factor_chips/ppermute | solution.py:30
  24.2 0.7 collective-permute-start.13
  26.2 6.2 %solve.1 = f32[128,256]{1,0:T(8,128)S(1)} custom-call(s32[5]{0:T(128)S(1)} %stack.75.place_ref, f32[256,128]{1,0:T(8,128)S(1)} %add_select_fusion.refs_0_, f32[320,128]{1,0:T(8,128)S(1)} %collective-permute-done.8.refs_1_, f32[320,128]{1,0:T(8,128)S(1)} %collective-permute-done.9.refs_2_, f32[320,128]{1,0:T(8,128)S(1)} %collective-permute-done.10.refs_3_, ...), custom_call_target="tpu_custom_call" | custom-call | flops 2147483648 | bytes 2097152 | tf_op jit(solution)/shard_map/solve/pallas_call | solution.py:312
  32.4 1.3 %collective-permute-start.16 = (f32[128,256]{1,0:T(8,128)S(1)}, f32[128,256]{1,0:T(8,128)S(1)}, u32[]{:S(2)}, u32[]{:S(2)}) collective-permute-start(f32[128,256]{1,0:T(8,128)S(1)} %solve.1), channel_id=1, source_target_pairs={{0,4},{1,5},{2,6},{3,7},{8,12},{9,13},{10,14},{11,15},{16,20},{17,... | collective-permute-start | bytes 393224 | tf_op jit(solution)/shard_map/errors_plane/ppermute | solution.py:30
  33.7 25.3 %collective-permute-done.16 = f32[128,256]{1,0:T(8,128)S(1)} collective-permute-done((f32[128,256]{1,0:T(8,128)S(1)}, f32[128,256]{1,0:T(8,128)S(1)}, u32[]{:S(2)}, u32[]{:S(2)}) %collective-permute-start.16) | collective-permute-done | bytes 131104 | tf_op jit(solution)/shard_map/errors_plane/ppermute | solution.py:30
  59.6 1.4 %collective-permute-start.22 = (f32[128,256]{1,0:T(8,128)S(1)}, f32[128,256]{1,0:T(8,128)S(1)}, u32[]{:S(2)}, u32[]{:S(2)}) collective-permute-start(f32[128,256]{1,0:T(8,128)S(1)} %broadcast_select_fusion.refs_0_), channel_id=1, source_target_pairs={{0,24},{1,25},{2,26},{3,27},{4,28},{5,29},{6,30},{7,31},{8,0},{9,1... | collective-permute-start | bytes 393224 | tf_op jit(solution)/shard_map/errors_near/ppermute | solution.py:30
  61.0 3.4 %collective-permute-start.21 = (f32[128,256]{1,0:T(8,128)S(1)}, f32[128,256]{1,0:T(8,128)S(1)}, u32[]{:S(2)}, u32[]{:S(2)}) collective-permute-start(f32[128,256]{1,0:T(8,128)S(1)} %broadcast_select_fusion.refs_0_), channel_id=1, source_target_pairs={{0,16},{1,17},{2,18},{3,19},{4,20},{5,21},{6,22},{7,23},{8,24},{9,... | collective-permute-start | bytes 393224 | tf_op jit(solution)/shard_map/errors_near/ppermute | solution.py:30
  64.5 2.6 %collective-permute-start.20 = (f32[128,256]{1,0:T(8,128)S(1)}, f32[128,256]{1,0:T(8,128)S(1)}, u32[]{:S(2)}, u32[]{:S(2)}) collective-permute-start(f32[128,256]{1,0:T(8,128)S(1)} %broadcast_select_fusion.refs_0_), channel_id=1, source_target_pairs={{0,8},{1,9},{2,10},{3,11},{4,12},{5,13},{6,14},{7,15},{8,16},{9,17... | collective-permute-start | bytes 393224 | tf_op jit(solution)/shard_map/errors_near/ppermute | solution.py:30
  67.1 1.0 collective-permute-start.18
  68.1 1.1 %collective-permute-start.17 = (f32[128,256]{1,0:T(8,128)S(1)}, f32[128,256]{1,0:T(8,128)S(1)}, u32[]{:S(2)}, u32[]{:S(2)}) collective-permute-start(f32[128,256]{1,0:T(8,128)S(1)} %broadcast_select_fusion.refs_0_), channel_id=1, source_target_pairs={{0,1},{1,2},{2,3},{3,0},{4,5},{5,6},{6,7},{7,4},{8,9},{9,10},{10,1... | collective-permute-start | bytes 393224 | tf_op jit(solution)/shard_map/errors_near/ppermute | solution.py:30
  69.1 5.7 %collective-permute-done.18.refs_2_ = f32[128,256]{1,0:T(8,128)S(1)} collective-permute-done((f32[128,256]{1,0:T(8,128)S(1)}, f32[128,256]{1,0:T(8,128)S(1)}, u32[]{:S(2)}, u32[]{:S(2)}) %collective-permute-start.18) | collective-permute-done | bytes 131104 | tf_op jit(solution)/shard_map/errors_near/ppermute | solution.py:30
  74.8 1.0 collective-permute-done.17.refs_1_
  76.1 1.7 %collective-permute-start.24 = (f32[3,64,256]{2,1,0:T(8,128)S(1)}, f32[3,64,256]{2,1,0:T(8,128)S(1)}, u32[]{:S(2)}, u32[]{:S(2)}) collective-permute-start(f32[3,64,256]{2,1,0:T(8,128)S(1)} %pad_maximum_fusion.2), channel_id=1, source_target_pairs={{0,16},{1,17},{2,18},{3,19},{4,20},{5,21},{6,22},{7,23},{8,24},{9,... | collective-permute-start | bytes 589832 | tf_op jit(solution)/shard_map/errors_far/ppermute | solution.py:30
  77.8 1.6 %collective-permute-start.23 = (f32[3,64,256]{2,1,0:T(8,128)S(1)}, f32[3,64,256]{2,1,0:T(8,128)S(1)}, u32[]{:S(2)}, u32[]{:S(2)}) collective-permute-start(f32[3,64,256]{2,1,0:T(8,128)S(1)} %pad_maximum_fusion.2), channel_id=1, source_target_pairs={{0,8},{1,9},{2,10},{3,11},{4,12},{5,13},{6,14},{7,15},{8,16},{9,17... | collective-permute-start | bytes 589832 | tf_op jit(solution)/shard_map/errors_far/ppermute | solution.py:30
  79.4 1.0 collective-permute-start.28
  81.0 6.2 %collective-permute-done.25.refs_2_ = f32[3,64,256]{2,1,0:T(8,128)S(1)} collective-permute-done((f32[3,64,256]{2,1,0:T(8,128)S(1)}, f32[3,64,256]{2,1,0:T(8,128)S(1)}, u32[]{:S(2)}, u32[]{:S(2)}) %collective-permute-start.25) | collective-permute-done | bytes 196640 | tf_op jit(solution)/shard_map/errors_far/ppermute | solution.py:30
  87.2 0.8 layout.1.spread_ref
  87.9 4.4 %update.2.refs_6_ = f32[8192,128]{1,0:T(8,128)} custom-call(s32[5]{0:T(128)S(1)} %stack.75.place_ref, f32[8192,128]{1,0:T(8,128)} %bitcast.62, bf16[1536,512]{1,0:T(8,128)(2,1)S(1)} %layout.1.spread_ref, s32[16,4,128]{2,1,0:T(4,128)S(1)} %fusion.6.target_ref.refs_7_, f32[128,256]{1,0:T(8,128)S(1)} %broadcast_select_fusion.refs_0_, ...), custom_call_target="tpu_custom_call" | custom-call | flops 1879048192 | bytes 3670016 | tf_op jit(solution)/shard_map/update/pallas_call | solution.py:226
  92.3 1.7 %collective-permute-done.26.refs_3_ = f32[3,64,256]{2,1,0:T(8,128)S(1)} collective-permute-done((f32[3,64,256]{2,1,0:T(8,128)S(1)}, f32[3,64,256]{2,1,0:T(8,128)S(1)}, u32[]{:S(2)}, u32[]{:S(2)}) %collective-permute-start.26) | collective-permute-done | bytes 196640 | tf_op jit(solution)/shard_map/errors_far/ppermute | solution.py:30
  94.1 5.0 %update.3 = f32[8192,128]{1,0:T(8,128)} custom-call(s32[5]{0:T(128)S(1)} %stack.75.place_ref, f32[8192,128]{1,0:T(8,128)} %bitcast.63, bf16[1536,512]{1,0:T(8,128)(2,1)S(1)} %layout.1.spread_ref, s32[16,4,128]{2,1,0:T(4,128)S(1)} %fusion.6.target_ref.refs_7_, f32[3,64,256]{2,1,0:T(8,128)S(1)} %collective-permute-done.23.refs_0_, ...), custom_call_target="tpu_custom_call", output_to_operand_aliasing={{}: (10, {})} | custom-call | flops 2415919104 | bytes 4718592 | tf_op jit(solution)/shard_map/update/pallas_call | solution.py:226
  (60 shorter events, 6.0 us)
Async XLA Ops:
  0.0 6.8 %copy-start.1 = (f32[4,16,4,128]{3,2,1,0:T(4,128)S(1)}, f32[4,16,4,128]{3,2,1,0:T(4,128)}, u32[]{:S(2)}) copy-start(f32[4,16,4,128]{3,2,1,0:T(4,128)} %param.4) | copy-start | bytes 393220
  0.0 6.7 %collective-permute-start = (f32[256,128]{1,0:T(8,128)}, f32[256,128]{1,0:T(8,128)S(1)}, u32[]{:S(2)}, u32[]{:S(2)}) collective-permute-start(f32[256,128]{1,0:T(8,128)} %bitcast.67), channel_id=1, source_target_pairs={{0,64},{1,65},{2,66},{3,67},{4,68},{5,69},{6,70},{7,71},{8,72},{9,... | collective-permute-start | bytes 393224 | tf_op jit(solution)/shard_map/triangle_rows/ppermute | solution.py:30
  2.8 2.2 %copy-start = (f32[2048,4,128]{2,1,0:T(4,128)S(1)}, f32[2048,4,128]{2,1,0:T(4,128)}, u32[]{:S(2)}) copy-start(f32[2048,4,128]{2,1,0:T(4,128)} %param.3) | copy-start | bytes 12582916
  6.8 2.8 %collective-permute-start.1 = (f32[2,64,128]{2,1,0:T(8,128)S(1)}, f32[2,64,128]{2,1,0:T(8,128)S(1)}, u32[]{:S(2)}, u32[]{:S(2)}) collective-permute-start(f32[2,64,128]{2,1,0:T(8,128)S(1)} %bitcast.76), channel_id=1, source_target_pairs={{0,128},{1,129},{2,130},{3,131},{32,160},{33,161},{34,162},{35,163... | collective-permute-start | bytes 196616 | tf_op jit(solution)/shard_map/triangle_pairs/ppermute | solution.py:30
  7.5 3.4 %collective-permute-start.6 = (f32[4,64,128]{2,1,0:T(8,128)S(1)}, f32[4,64,128]{2,1,0:T(8,128)S(1)}, u32[]{:S(2)}, u32[]{:S(2)}) collective-permute-start(f32[4,64,128]{2,1,0:T(8,128)S(1)} %get-tuple-element.45), channel_id=1, source_target_pairs={{0,16},{1,17},{2,18},{3,19},{32,48},{33,49},{34,50},{35,51},{64,80... | collective-permute-start | bytes 393224 | tf_op jit(solution)/shard_map/slab_x/ppermute | solution.py:30
  8.2 3.5 %collective-permute-start.5 = (f32[4,64,128]{2,1,0:T(8,128)S(1)}, f32[4,64,128]{2,1,0:T(8,128)S(1)}, u32[]{:S(2)}, u32[]{:S(2)}) collective-permute-start(f32[4,64,128]{2,1,0:T(8,128)S(1)} %get-tuple-element.46), channel_id=1, source_target_pairs={{0,8},{1,9},{2,10},{3,11},{32,40},{33,41},{34,42},{35,43},{64,72},... | collective-permute-start | bytes 393224 | tf_op jit(solution)/shard_map/slab_x/ppermute | solution.py:30
  8.9 4.3 %collective-permute-start.7 = (f32[4,64,128]{2,1,0:T(8,128)S(1)}, f32[4,64,128]{2,1,0:T(8,128)S(1)}, u32[]{:S(2)}, u32[]{:S(2)}) collective-permute-start(f32[4,64,128]{2,1,0:T(8,128)S(1)} %get-tuple-element.47), channel_id=1, source_target_pairs={{0,24},{1,25},{2,26},{3,27},{32,56},{33,57},{34,58},{35,59},{64,88... | collective-permute-start | bytes 393224 | tf_op jit(solution)/shard_map/slab_x/ppermute | solution.py:30
  9.6 3.7 %collective-permute-start.4 = (f32[256,128]{1,0:T(8,128)S(1)}, f32[256,128]{1,0:T(8,128)S(1)}, u32[]{:S(2)}, u32[]{:S(2)}) collective-permute-start(f32[256,128]{1,0:T(8,128)S(1)} %bitcast.72), channel_id=1, source_target_pairs={{0,24},{1,25},{2,26},{3,27},{32,56},{33,57},{34,58},{35,59},{64,88... | collective-permute-start | bytes 393224 | tf_op jit(solution)/shard_map/triangle_x/ppermute | solution.py:30
  10.3 3.0 %collective-permute-start.3 = (f32[256,128]{1,0:T(8,128)S(1)}, f32[256,128]{1,0:T(8,128)S(1)}, u32[]{:S(2)}, u32[]{:S(2)}) collective-permute-start(f32[256,128]{1,0:T(8,128)S(1)} %bitcast.73), channel_id=1, source_target_pairs={{0,16},{1,17},{2,18},{3,19},{32,48},{33,49},{34,50},{35,51},{64,80... | collective-permute-start | bytes 393224 | tf_op jit(solution)/shard_map/triangle_x/ppermute | solution.py:30
  11.0 2.3 %collective-permute-start.2 = (f32[256,128]{1,0:T(8,128)S(1)}, f32[256,128]{1,0:T(8,128)S(1)}, u32[]{:S(2)}, u32[]{:S(2)}) collective-permute-start(f32[256,128]{1,0:T(8,128)S(1)} %bitcast.74), channel_id=1, source_target_pairs={{0,8},{1,9},{2,10},{3,11},{32,40},{33,41},{34,42},{35,43},{64,72},... | collective-permute-start | bytes 393224 | tf_op jit(solution)/shard_map/triangle_x/ppermute | solution.py:30
  11.7 12.4 %collective-permute-start.11 = (f32[2,256,128]{2,1,0:T(8,128)S(1)}, f32[2,256,128]{2,1,0:T(8,128)S(1)}, u32[]{:S(2)}, u32[]{:S(2)}) collective-permute-start(f32[2,256,128]{2,1,0:T(8,128)S(1)} %pad_maximum_fusion.1.refs_0_), channel_id=1, source_target_pairs={{0,128},{1,129},{2,130},{3,131},{4,132},{5,133},{6,134},{7,135},{8... | collective-permute-start | bytes 786440 | tf_op jit(solution)/shard_map/factor_chips/ppermute | solution.py:30
  13.4 10.7 %collective-permute-start.10 = (f32[320,128]{1,0:T(8,128)S(1)}, f32[320,128]{1,0:T(8,128)S(1)}, u32[]{:S(2)}, u32[]{:S(2)}) collective-permute-start(f32[320,128]{1,0:T(8,128)S(1)} %get-tuple-element.52), channel_id=1, source_target_pairs={{0,3},{1,0},{2,1},{3,2},{8,11},{9,8},{10,9},{11,10},{16,19},{17,16... | collective-permute-start | bytes 491528 | tf_op jit(solution)/shard_map/triangle_y/ppermute | solution.py:30
  14.1 10.0 %collective-permute-start.9 = (f32[320,128]{1,0:T(8,128)S(1)}, f32[320,128]{1,0:T(8,128)S(1)}, u32[]{:S(2)}, u32[]{:S(2)}) collective-permute-start(f32[320,128]{1,0:T(8,128)S(1)} %get-tuple-element.53), channel_id=1, source_target_pairs={{0,2},{1,3},{2,0},{3,1},{8,10},{9,11},{10,8},{11,9},{16,18},{17,19... | collective-permute-start | bytes 491528 | tf_op jit(solution)/shard_map/triangle_y/ppermute | solution.py:30
  14.8 9.4 %collective-permute-start.8 = (f32[320,128]{1,0:T(8,128)S(1)}, f32[320,128]{1,0:T(8,128)S(1)}, u32[]{:S(2)}, u32[]{:S(2)}) collective-permute-start(f32[320,128]{1,0:T(8,128)S(1)} %get-tuple-element.54), channel_id=1, source_target_pairs={{0,1},{1,2},{2,3},{3,0},{8,9},{9,10},{10,11},{11,8},{16,17},{17,18... | collective-permute-start | bytes 491528 | tf_op jit(solution)/shard_map/triangle_y/ppermute | solution.py:30
  24.2 2.0 %collective-permute-start.13 = (f32[3,256,128]{2,1,0:T(8,128)S(1)}, f32[3,256,128]{2,1,0:T(8,128)S(1)}, u32[]{:S(2)}, u32[]{:S(2)}) collective-permute-start(f32[3,256,128]{2,1,0:T(8,128)S(1)} %pad_maximum_fusion), channel_id=1, source_target_pairs={{0,32},{1,33},{2,34},{3,35},{8,40},{9,41},{10,42},{11,43},{16,48},... | collective-permute-start | bytes 1179656 | tf_op jit(solution)/shard_map/triangle_core/ppermute | solution.py:30
  24.9 1.3 %collective-permute-start.12 = (f32[256,128]{1,0:T(8,128)S(1)}, f32[256,128]{1,0:T(8,128)S(1)}, u32[]{:S(2)}, u32[]{:S(2)}) collective-permute-start(f32[256,128]{1,0:T(8,128)S(1)} %add_select_fusion.refs_0_), channel_id=1, source_target_pairs={{0,32},{1,33},{2,34},{3,35},{8,40},{9,41},{10,42},{11,43},{16,48},... | collective-permute-start | bytes 393224 | tf_op jit(solution)/shard_map/triangle_core/ppermute | solution.py:30
  25.6 6.8 %collective-permute-start.14 = (f32[2,256,128]{2,1,0:T(8,128)S(1)}, f32[2,256,128]{2,1,0:T(8,128)S(1)}, u32[]{:S(2)}, u32[]{:S(2)}) collective-permute-start(f32[2,256,128]{2,1,0:T(8,128)S(1)} %pad_maximum_fusion.1.refs_0_), channel_id=1, source_target_pairs={{0,32},{1,33},{2,34},{3,35},{4,36},{5,37},{6,38},{7,39},{8,40},{9,... | collective-permute-start | bytes 786440 | tf_op jit(solution)/shard_map/factor_core/ppermute | solution.py:30
  25.7 6.7 %collective-permute-start.15 = (f32[2,256,128]{2,1,0:T(8,128)S(1)}, f32[2,256,128]{2,1,0:T(8,128)S(1)}, u32[]{:S(2)}, u32[]{:S(2)}) collective-permute-start(f32[2,256,128]{2,1,0:T(8,128)S(1)} %collective-permute-done.11.refs_1_), channel_id=1, source_target_pairs={{0,32},{1,33},{2,34},{3,35},{4,36},{5,37},{6,38},{7,39},{8,40},{9,... | collective-permute-start | bytes 786440 | tf_op jit(solution)/shard_map/factor_core/ppermute | solution.py:30
  32.4 26.6 %collective-permute-start.16 = (f32[128,256]{1,0:T(8,128)S(1)}, f32[128,256]{1,0:T(8,128)S(1)}, u32[]{:S(2)}, u32[]{:S(2)}) collective-permute-start(f32[128,256]{1,0:T(8,128)S(1)} %solve.1), channel_id=1, source_target_pairs={{0,4},{1,5},{2,6},{3,7},{8,12},{9,13},{10,14},{11,15},{16,20},{17,... | collective-permute-start | bytes 393224 | tf_op jit(solution)/shard_map/errors_plane/ppermute | solution.py:30
  59.0 9.0 %collective-permute-start.19 = (f32[128,256]{1,0:T(8,128)S(1)}, f32[128,256]{1,0:T(8,128)S(1)}, u32[]{:S(2)}, u32[]{:S(2)}) collective-permute-start(f32[128,256]{1,0:T(8,128)S(1)} %broadcast_select_fusion.refs_0_), channel_id=1, source_target_pairs={{0,3},{1,0},{2,1},{3,2},{4,7},{5,4},{6,5},{7,6},{8,11},{9,8},{10,9... | collective-permute-start | bytes 393224 | tf_op jit(solution)/shard_map/errors_near/ppermute | solution.py:30
  59.6 18.2 %collective-permute-start.22 = (f32[128,256]{1,0:T(8,128)S(1)}, f32[128,256]{1,0:T(8,128)S(1)}, u32[]{:S(2)}, u32[]{:S(2)}) collective-permute-start(f32[128,256]{1,0:T(8,128)S(1)} %broadcast_select_fusion.refs_0_), channel_id=1, source_target_pairs={{0,24},{1,25},{2,26},{3,27},{4,28},{5,29},{6,30},{7,31},{8,0},{9,1... | collective-permute-start | bytes 393224 | tf_op jit(solution)/shard_map/errors_near/ppermute | solution.py:30
  61.0 18.3 %collective-permute-start.21 = (f32[128,256]{1,0:T(8,128)S(1)}, f32[128,256]{1,0:T(8,128)S(1)}, u32[]{:S(2)}, u32[]{:S(2)}) collective-permute-start(f32[128,256]{1,0:T(8,128)S(1)} %broadcast_select_fusion.refs_0_), channel_id=1, source_target_pairs={{0,16},{1,17},{2,18},{3,19},{4,20},{5,21},{6,22},{7,23},{8,24},{9,... | collective-permute-start | bytes 393224 | tf_op jit(solution)/shard_map/errors_near/ppermute | solution.py:30
  64.5 14.9 %collective-permute-start.20 = (f32[128,256]{1,0:T(8,128)S(1)}, f32[128,256]{1,0:T(8,128)S(1)}, u32[]{:S(2)}, u32[]{:S(2)}) collective-permute-start(f32[128,256]{1,0:T(8,128)S(1)} %broadcast_select_fusion.refs_0_), channel_id=1, source_target_pairs={{0,8},{1,9},{2,10},{3,11},{4,12},{5,13},{6,14},{7,15},{8,16},{9,17... | collective-permute-start | bytes 393224 | tf_op jit(solution)/shard_map/errors_near/ppermute | solution.py:30
  67.1 7.7 %collective-permute-start.18 = (f32[128,256]{1,0:T(8,128)S(1)}, f32[128,256]{1,0:T(8,128)S(1)}, u32[]{:S(2)}, u32[]{:S(2)}) collective-permute-start(f32[128,256]{1,0:T(8,128)S(1)} %broadcast_select_fusion.refs_0_), channel_id=1, source_target_pairs={{0,2},{1,3},{2,0},{3,1},{4,6},{5,7},{6,4},{7,5},{8,10},{9,11},{10,... | collective-permute-start | bytes 393224 | tf_op jit(solution)/shard_map/errors_near/ppermute | solution.py:30
  68.1 7.7 %collective-permute-start.17 = (f32[128,256]{1,0:T(8,128)S(1)}, f32[128,256]{1,0:T(8,128)S(1)}, u32[]{:S(2)}, u32[]{:S(2)}) collective-permute-start(f32[128,256]{1,0:T(8,128)S(1)} %broadcast_select_fusion.refs_0_), channel_id=1, source_target_pairs={{0,1},{1,2},{2,3},{3,0},{4,5},{5,6},{6,7},{7,4},{8,9},{9,10},{10,1... | collective-permute-start | bytes 393224 | tf_op jit(solution)/shard_map/errors_near/ppermute | solution.py:30
  75.8 11.4 %collective-permute-start.25 = (f32[3,64,256]{2,1,0:T(8,128)S(1)}, f32[3,64,256]{2,1,0:T(8,128)S(1)}, u32[]{:S(2)}, u32[]{:S(2)}) collective-permute-start(f32[3,64,256]{2,1,0:T(8,128)S(1)} %pad_maximum_fusion.2), channel_id=1, source_target_pairs={{0,24},{1,25},{2,26},{3,27},{4,28},{5,29},{6,30},{7,31},{8,0},{9,1... | collective-permute-start | bytes 589832 | tf_op jit(solution)/shard_map/errors_far/ppermute | solution.py:30
  76.1 16.2 %collective-permute-start.24 = (f32[3,64,256]{2,1,0:T(8,128)S(1)}, f32[3,64,256]{2,1,0:T(8,128)S(1)}, u32[]{:S(2)}, u32[]{:S(2)}) collective-permute-start(f32[3,64,256]{2,1,0:T(8,128)S(1)} %pad_maximum_fusion.2), channel_id=1, source_target_pairs={{0,16},{1,17},{2,18},{3,19},{4,20},{5,21},{6,22},{7,23},{8,24},{9,... | collective-permute-start | bytes 589832 | tf_op jit(solution)/shard_map/errors_far/ppermute | solution.py:30
  77.8 14.5 %collective-permute-start.23 = (f32[3,64,256]{2,1,0:T(8,128)S(1)}, f32[3,64,256]{2,1,0:T(8,128)S(1)}, u32[]{:S(2)}, u32[]{:S(2)}) collective-permute-start(f32[3,64,256]{2,1,0:T(8,128)S(1)} %pad_maximum_fusion.2), channel_id=1, source_target_pairs={{0,8},{1,9},{2,10},{3,11},{4,12},{5,13},{6,14},{7,15},{8,16},{9,17... | collective-permute-start | bytes 589832 | tf_op jit(solution)/shard_map/errors_far/ppermute | solution.py:30
  79.4 12.9 %collective-permute-start.28 = (f32[3,64,256]{2,1,0:T(8,128)S(1)}, f32[3,64,256]{2,1,0:T(8,128)S(1)}, u32[]{:S(2)}, u32[]{:S(2)}) collective-permute-start(f32[3,64,256]{2,1,0:T(8,128)S(1)} %pad_maximum_fusion.3), channel_id=1, source_target_pairs={{0,3},{1,0},{2,1},{3,2},{4,7},{5,4},{6,5},{7,6},{8,11},{9,8},{10,9... | collective-permute-start | bytes 589832 | tf_op jit(solution)/shard_map/errors_far/ppermute | solution.py:30
  80.4 11.9 %collective-permute-start.27 = (f32[3,64,256]{2,1,0:T(8,128)S(1)}, f32[3,64,256]{2,1,0:T(8,128)S(1)}, u32[]{:S(2)}, u32[]{:S(2)}) collective-permute-start(f32[3,64,256]{2,1,0:T(8,128)S(1)} %pad_maximum_fusion.3), channel_id=1, source_target_pairs={{0,2},{1,3},{2,0},{3,1},{4,6},{5,7},{6,4},{7,5},{8,10},{9,11},{10,... | collective-permute-start | bytes 589832 | tf_op jit(solution)/shard_map/errors_far/ppermute | solution.py:30
  87.2 6.9 %collective-permute-start.26 = (f32[3,64,256]{2,1,0:T(8,128)S(1)}, f32[3,64,256]{2,1,0:T(8,128)S(1)}, u32[]{:S(2)}, u32[]{:S(2)}) collective-permute-start(f32[3,64,256]{2,1,0:T(8,128)S(1)} %pad_maximum_fusion.3), channel_id=1, source_target_pairs={{0,1},{1,2},{2,3},{3,0},{4,5},{5,6},{6,7},{7,4},{8,9},{9,10},{10,1... | collective-permute-start | bytes 589832 | tf_op jit(solution)/shard_map/errors_far/ppermute | solution.py:30

commit v3 on v2

--- a/solution.py
+++ b/solution.py
@@ -85,33 +85,42 @@
         out_ref[group] = dot(pick, high, NT) + (dot(pick, mid, NT) + dot(pick, low, NT))
 
 
-def solve_kernel(place_ref, *refs):
-    mine, others, far = refs[0:NY], refs[NY], refs[NY + 1]
-    w_ref, target_ref, out_ref, tri_ref, slab_ref = refs[NY + 2 :]
+def columns_kernel(place_ref, tri_ref, other_ref, slabs_ref, target_ref, *refs):
+    out_refs, full_ref = refs[:NY], refs[NY]
     x, y, zl, core = place_ref[0], place_ref[1], place_ref[2], place_ref[3]
+    inner = BW // (2 * NZL)
+    for q, half in enumerate((tri_ref, other_ref)):
+        for j in range(NZL):
+            owner = ((zl ^ j) * 2 + (core ^ q)) * inner
+            for b in range(NB):
+                full_ref[pl.ds(pl.multiple_of(b * BW + owner, inner), inner), :] = half[
+                    (j * NB + b) * inner : (j * NB + b + 1) * inner, :
+                ]
+    rows = lax.broadcasted_iota(jnp.int32, (ACT, BW), 0) + y * ACT
+    tri = full_ref[...]
+    high, rest = split(tri)
+    mid, low = split(tri - high.astype(F32))
+    for s, out_ref in enumerate(out_refs):
+        other = (y + s) & (NY - 1)
+        pick = (rows == target_ref[other * NX + x, pl.ds(y, 1), :]).astype(F32).astype(BF16)
+        out_ref[:, 0 : 4 * BW] = dot(pick, high, NT) + (dot(pick, mid, NT) + dot(pick, low, NT))
+        out_ref[:, 4 * BW : 5 * BW] = slabs_ref[other]
+
+
+def solve_kernel(place_ref, p0, p1, p2, p3, target_ref, out_ref, tri_ref, slab_ref):
+    x, y = place_ref[0], place_ref[1]
     group = y * NX + x
-    inner = BW // (2 * NZL)
-    for s in range(NY):
+    for s, piece in enumerate((p0, p1, p2, p3)):
         block = (y + (NY - s)) & (NY - 1)
-        for q, piece in ((0, mine[s]), (1, others if s == 0 else far.at[s - 1])):
-            for j in range(NZL):
-                owner = ((zl ^ j) * 2 + (core ^ q)) * inner
-                for b in range(NB):
-                    tri_ref[block, pl.ds(pl.multiple_of(b * BW + owner, inner), inner), :] = piece[
-                        (j * NB + b) * inner : (j * NB + b + 1) * inner, :
-                    ]
-        slab_ref[pl.ds(pl.multiple_of(block * ACT, ACT), ACT), :] = (
-            w_ref[...] if s == 0 else mine[s][NB * BW // 2 :, :]
-        )
+        here = pl.ds(pl.multiple_of(block * ACT, ACT), ACT)
+        tri_ref[here, :] = piece[:, 0 : 4 * BW]
+        slab_ref[here, :] = piece[:, 4 * BW : 5 * BW]
     rows = lax.broadcasted_iota(jnp.int32, (KACT, BW), 0)
     pick = jnp.concatenate(
         [(rows == target_ref[group, b : b + 1, :]).astype(F32).astype(BF16) for b in range(NB)], axis=1
     )
-    full = jnp.concatenate([tri_ref[b] for b in range(NB)], axis=1)
-    high, low = split(full)
-    high = dot(pick, high).astype(BF16)
-    low = dot(pick, low).astype(BF16)
-    active = dot(high, pick, NT) + dot(low, pick, NT)
+    high, low = split(tri_ref[...])
+    active = (dot(high, pick, NT) + dot(low, pick, NT)).T
     row_id = lax.broadcasted_iota(jnp.int32, (KACT, KACT), 0)
     col_ids = lax.broadcasted_iota(jnp.int32, (KACT, KACT), 1)
     diagonal = jnp.where(row_id == col_ids, active, 0.0)
@@ -294,16 +303,21 @@
 
     with jax.named_scope("triangle_y"):
         tri = jnp.where(x == 0, tri, moved[0] + moved[1] + moved[2])
-        mixed = []
-        for s in (1, 2, 3):
-            piece = lax.dynamic_index_in_dim(slabs, (y + s) & 3, 0, keepdims=False)
-            mixed.append(shift(jnp.concatenate([tri, piece]), 0, s, (0,)))
-        slab = lax.dynamic_index_in_dim(slabs, y, 0, keepdims=False)
+        other = swap_core(tri)
+        mixed = pl.pallas_call(
+            columns_kernel,
+            out_shape=[jax.ShapeDtypeStruct((ACT, 5 * BW), F32)] * NY,
+            in_specs=[SMEM] + [whole(v.shape) for v in (tri, other, slabs, target)],
+            out_specs=[whole((ACT, 5 * BW))] * NY,
+            grid=(1,),
+            scratch_shapes=[pltpu.VMEM((NB * BW, BW), F32)],
+            compiler_params=pltpu.CompilerParams(vmem_limit_bytes=16 << 20),
+            cost_estimate=pl.CostEstimate(flops=2**28, bytes_accessed=2**20, transcendentals=0),
+        )(place, tri, other, slabs, target)
+        mixed = [mixed[0]] + [shift(mixed[s], 0, s) for s in (1, 2, 3)]
 
     with jax.named_scope("triangle_core"):
-        tri, mixed, chips = barrier((tri, mixed, chips))
-        others = swap_core(jnp.stack([piece[: NB * BW // 2] for piece in mixed]), (0,))
-        other = swap_core(tri, (0,))
+        mixed, chips = barrier((mixed, chips))
 
     with jax.named_scope("factor_core"):
         other_chips = [swap_core(piece) for piece in chips]
@@ -312,14 +326,16 @@
         errors = pl.pallas_call(
             solve_kernel,
             out_shape=jax.ShapeDtypeStruct((BW, KACT), F32),
-            in_specs=[SMEM, whole(tri.shape)] + [whole(mixed[0].shape)] * 3
-            + [whole(v.shape) for v in (other, others, slab, target)],
+            in_specs=[SMEM] + [whole(v.shape) for v in (*mixed, target)],
             out_specs=whole((BW, KACT)),
             grid=(1,),
-            scratch_shapes=[pltpu.VMEM((NB, NB * BW, BW), F32), pltpu.VMEM((KACT, BW), F32)],
+            scratch_shapes=[
+                pltpu.VMEM((KACT, NB * BW), F32),
+                pltpu.VMEM((KACT, BW), F32),
+            ],
             compiler_params=pltpu.CompilerParams(vmem_limit_bytes=32 << 20),
             cost_estimate=pl.CostEstimate(flops=2**31, bytes_accessed=2**21, transcendentals=0),
-        )(place, tri, *mixed, other, others, slab, target)
+        )(place, *mixed, target)
 
     with jax.named_scope("errors_plane"):
         errors, other_chips = barrier((errors, other_chips))

time: 99.8 us -> 92 us (0.922); the launches traced: 99.2 us -> 90.4 us
  waiting for transfers between devices: 48.6 us -> 36.8 us
  starting transfers between devices: 27.7 us -> 29.9 us
    ppermute x29 -> x28, waiting for transfers between devices: 48.6 us -> 36.8 us  [permute(): return lax.ppermute(value, ('row', 'col'), pairs)]
    ppermute x29 -> x28, starting transfers between devices: 27.7 us -> 29.9 us  [permute(): return lax.ppermute(value, ('row', 'col'), pairs)]
    pallas_call x0 -> x1, Pallas kernels: none -> 1.25 us  [local(): pl.pallas_call(columns_kernel, out_shape=[jax.ShapeDtypeStruct((ACT, 5 *...]
  transfers between devices with their start and end apart: 29 -> 28, of which waited for: 6 -> 8; matrix products, arithmetic and copies ran while one was open for 2% -> 2% of each run, Pallas kernels for 13% -> 15%
where the time goes in v3:
time: 92 us; the launch traced here: 90.4 us
  waiting for transfers between devices  36.8 us (40%)
  starting transfers between devices  29.9 us (32%)
  Pallas kernels  18.9 us (21%)
  local copies, waits for them, and re-layouts  2.35 us (3%)
  other arithmetic  1.81 us (2%)
    ppermute x28, waiting for transfers between devices, permute(): return lax.ppermute(value, ('row', 'col'), pairs)  36.8 us
    ppermute x28, starting transfers between devices, permute(): return lax.ppermute(value, ('row', 'col'), pairs)  29.9 us
    pallas_call x2, Pallas kernels, update(): pl.pallas_call(functools.partial(update_kernel, pieces=(errors, plan, pla...  9.33 us
    pallas_call x1, Pallas kernels, local(): pl.pallas_call(solve_kernel, out_shape=jax.ShapeDtypeStruct((BW, KACT), F...  5.91 us
    unnamed x4, local copies, waits for them, and re-layouts  2.21 us
  transfers between devices with their start and end apart: 28, of which 8 were waited for; matrix products, arithmetic and copies ran while one was open for 2% of the time, Pallas kernels for 15%

profile of v3, /device:TPU:198, one launch (start us, length us, event | category | flops | bytes accessed | tf_op | source)
XLA Modules:
  0.0 90.4 jit_solution(17341826639269045909)
XLA Ops:
  0.0 1.0 %collective-permute-start = (f32[256,128]{1,0:T(8,128)}, f32[256,128]{1,0:T(8,128)S(1)}, u32[]{:S(2)}, u32[]{:S(2)}) collective-permute-start(f32[256,128]{1,0:T(8,128)} %bitcast.53), channel_id=1, source_target_pairs={{0,64},{1,65},{2,66},{3,67},{4,68},{5,69},{6,70},{7,71},{8,72},{9,... | collective-permute-start | bytes 393224 | tf_op jit(solution)/shard_map/triangle_rows/ppermute | solution.py:30
  1.0 0.8 subtract_convert_fusion
  1.9 0.8 fusion.6.target_ref
  2.9 2.2 %copy-done = f32[2048,4,128]{2,1,0:T(4,128)S(1)} copy-done((f32[2048,4,128]{2,1,0:T(4,128)S(1)}, f32[2048,4,128]{2,1,0:T(4,128)}, u32[]{:S(2)}) %copy-start) | copy-done | bytes 4194328
  5.0 1.7 %compact.1 = f32[16,64,128]{2,1,0:T(8,128)S(1)} custom-call(s32[5]{0:T(128)S(1)} %stack.63.place_ref, f32[8192,128]{1,0:T(8,128)S(1)} %bitcast.50, s32[16,4,128]{2,1,0:T(4,128)S(1)} %fusion.6.target_ref), custom_call_target="tpu_custom_call" | custom-call | flops 1073741824 | bytes 16777216 | tf_op jit(solution)/shard_map/compact/pallas_call | solution.py:275
  8.9 0.7 collective-permute-start.2
  11.0 0.7 collective-permute-start.8
  11.7 1.5 %collective-permute-start.12 = (f32[2,256,128]{2,1,0:T(8,128)S(1)}, f32[2,256,128]{2,1,0:T(8,128)S(1)}, u32[]{:S(2)}, u32[]{:S(2)}) collective-permute-start(f32[2,256,128]{2,1,0:T(8,128)S(1)} %pad_maximum_fusion.refs_0_), channel_id=1, source_target_pairs={{0,128},{1,129},{2,130},{3,131},{4,132},{5,133},{6,134},{7,135},{8... | collective-permute-start | bytes 786440 | tf_op jit(solution)/shard_map/factor_chips/ppermute | solution.py:30
  13.4 1.3 %collective-permute-done.5.other_ref = f32[256,128]{1,0:T(8,128)S(1)} collective-permute-done((f32[256,128]{1,0:T(8,128)S(1)}, f32[256,128]{1,0:T(8,128)S(1)}, u32[]{:S(2)}, u32[]{:S(2)}) %collective-permute-start.5) | collective-permute-done | bytes 131104 | tf_op jit(solution)/shard_map/triangle_y/ppermute | solution.py:30
  14.7 1.3 %triangle_y.1 = (f32[64,640]{1,0:T(8,128)S(1)}, f32[64,640]{1,0:T(8,128)S(1)}, f32[64,640]{1,0:T(8,128)S(1)}, f32[64,640]{1,0:T(8,128)S(1)}) custom-call(s32[5]{0:T(128)S(1)} %stack.63.place_ref, f32[256,128]{1,0:T(8,128)S(1)} %add_select_fusion.tri_ref, f32[256,128]{1,0:T(8,128)S(1)} %collective-permute-done.5.other_ref, f32[4,64,128]{2,1,0:T(8,128)S(1)} %fusion.slabs_ref, ...), custom_call_target="tpu_custom_call" | custom-call | flops 268435456 | bytes 1048576 | tf_op jit(solution)/shard_map/triangle_y/pallas_call | solution.py:307
  15.9 1.7 %collective-permute-start.9 = (f32[64,640]{1,0:T(8,128)S(1)}, f32[64,640]{1,0:T(8,128)S(1)}, u32[]{:S(2)}, u32[]{:S(2)}) collective-permute-start(f32[64,640]{1,0:T(8,128)S(1)} %get-tuple-element.33), channel_id=1, source_target_pairs={{0,1},{1,2},{2,3},{3,0},{4,5},{5,6},{6,7},{7,4},{8,9},{9,10},{10,1... | collective-permute-start | bytes 491528 | tf_op jit(solution)/shard_map/triangle_y/ppermute | solution.py:30
  17.6 2.9 %collective-permute-start.10 = (f32[64,640]{1,0:T(8,128)S(1)}, f32[64,640]{1,0:T(8,128)S(1)}, u32[]{:S(2)}, u32[]{:S(2)}) collective-permute-start(f32[64,640]{1,0:T(8,128)S(1)} %get-tuple-element.34), channel_id=1, source_target_pairs={{0,2},{1,3},{2,0},{3,1},{4,6},{5,7},{6,4},{7,5},{8,10},{9,11},{10,... | collective-permute-start | bytes 491528 | tf_op jit(solution)/shard_map/triangle_y/ppermute | solution.py:30
  20.5 1.3 %collective-permute-start.11 = (f32[64,640]{1,0:T(8,128)S(1)}, f32[64,640]{1,0:T(8,128)S(1)}, u32[]{:S(2)}, u32[]{:S(2)}) collective-permute-start(f32[64,640]{1,0:T(8,128)S(1)} %get-tuple-element.35), channel_id=1, source_target_pairs={{0,3},{1,0},{2,1},{3,2},{4,7},{5,4},{6,5},{7,6},{8,11},{9,8},{10,9... | collective-permute-start | bytes 491528 | tf_op jit(solution)/shard_map/triangle_y/ppermute | solution.py:30
  21.8 2.3 %collective-permute-done.12.refs_1_ = f32[2,256,128]{2,1,0:T(8,128)S(1)} collective-permute-done((f32[2,256,128]{2,1,0:T(8,128)S(1)}, f32[2,256,128]{2,1,0:T(8,128)S(1)}, u32[]{:S(2)}, u32[]{:S(2)}) %collective-permute-start.12) | collective-permute-done | bytes 262176 | tf_op jit(solution)/shard_map/factor_chips/ppermute | solution.py:30
  24.1 4.1 %collective-permute-done.10.p2 = f32[64,640]{1,0:T(8,128)S(1)} collective-permute-done((f32[64,640]{1,0:T(8,128)S(1)}, f32[64,640]{1,0:T(8,128)S(1)}, u32[]{:S(2)}, u32[]{:S(2)}) %collective-permute-start.10) | collective-permute-done | bytes 163872 | tf_op jit(solution)/shard_map/triangle_y/ppermute | solution.py:30
  28.7 5.9 %solve.1 = f32[128,256]{1,0:T(8,128)S(1)} custom-call(s32[5]{0:T(128)S(1)} %stack.63.place_ref, f32[64,640]{1,0:T(8,128)S(1)} %get-tuple-element.39.p0, f32[64,640]{1,0:T(8,128)S(1)} %collective-permute-done.9.p1, f32[64,640]{1,0:T(8,128)S(1)} %collective-permute-done.10.p2, f32[64,640]{1,0:T(8,128)S(1)} %collective-permute-done.11.p3, ...), custom_call_target="tpu_custom_call" | custom-call | flops 2147483648 | bytes 2097152 | tf_op jit(solution)/shard_map/solve/pallas_call | solution.py:326
  34.7 1.3 %collective-permute-start.15 = (f32[128,256]{1,0:T(8,128)S(1)}, f32[128,256]{1,0:T(8,128)S(1)}, u32[]{:S(2)}, u32[]{:S(2)}) collective-permute-start(f32[128,256]{1,0:T(8,128)S(1)} %solve.1), channel_id=1, source_target_pairs={{0,4},{1,5},{2,6},{3,7},{8,12},{9,13},{10,14},{11,15},{16,20},{17,... | collective-permute-start | bytes 393224 | tf_op jit(solution)/shard_map/errors_plane/ppermute | solution.py:30
  36.0 17.5 %collective-permute-done.15 = f32[128,256]{1,0:T(8,128)S(1)} collective-permute-done((f32[128,256]{1,0:T(8,128)S(1)}, f32[128,256]{1,0:T(8,128)S(1)}, u32[]{:S(2)}, u32[]{:S(2)}) %collective-permute-start.15) | collective-permute-done | bytes 131104 | tf_op jit(solution)/shard_map/errors_plane/ppermute | solution.py:30
  53.5 2.6 %collective-permute-start.18 = (f32[128,256]{1,0:T(8,128)S(1)}, f32[128,256]{1,0:T(8,128)S(1)}, u32[]{:S(2)}, u32[]{:S(2)}) collective-permute-start(f32[128,256]{1,0:T(8,128)S(1)} %broadcast_select_fusion.refs_0_), channel_id=1, source_target_pairs={{0,3},{1,0},{2,1},{3,2},{4,7},{5,4},{6,5},{7,6},{8,11},{9,8},{10,9... | collective-permute-start | bytes 393224 | tf_op jit(solution)/shard_map/errors_near/ppermute | solution.py:30
  56.4 3.1 %collective-permute-start.20 = (f32[128,256]{1,0:T(8,128)S(1)}, f32[128,256]{1,0:T(8,128)S(1)}, u32[]{:S(2)}, u32[]{:S(2)}) collective-permute-start(f32[128,256]{1,0:T(8,128)S(1)} %broadcast_select_fusion.refs_0_), channel_id=1, source_target_pairs={{0,16},{1,17},{2,18},{3,19},{4,20},{5,21},{6,22},{7,23},{8,24},{9,... | collective-permute-start | bytes 393224 | tf_op jit(solution)/shard_map/errors_near/ppermute | solution.py:30
  59.6 1.8 %collective-permute-start.19 = (f32[128,256]{1,0:T(8,128)S(1)}, f32[128,256]{1,0:T(8,128)S(1)}, u32[]{:S(2)}, u32[]{:S(2)}) collective-permute-start(f32[128,256]{1,0:T(8,128)S(1)} %broadcast_select_fusion.refs_0_), channel_id=1, source_target_pairs={{0,8},{1,9},{2,10},{3,11},{4,12},{5,13},{6,14},{7,15},{8,16},{9,17... | collective-permute-start | bytes 393224 | tf_op jit(solution)/shard_map/errors_near/ppermute | solution.py:30
  61.7 1.3 %collective-permute-start.16 = (f32[128,256]{1,0:T(8,128)S(1)}, f32[128,256]{1,0:T(8,128)S(1)}, u32[]{:S(2)}, u32[]{:S(2)}) collective-permute-start(f32[128,256]{1,0:T(8,128)S(1)} %broadcast_select_fusion.refs_0_), channel_id=1, source_target_pairs={{0,1},{1,2},{2,3},{3,0},{4,5},{5,6},{6,7},{7,4},{8,9},{9,10},{10,1... | collective-permute-start | bytes 393224 | tf_op jit(solution)/shard_map/errors_near/ppermute | solution.py:30
  63.1 4.9 %collective-permute-done.17.refs_2_ = f32[128,256]{1,0:T(8,128)S(1)} collective-permute-done((f32[128,256]{1,0:T(8,128)S(1)}, f32[128,256]{1,0:T(8,128)S(1)}, u32[]{:S(2)}, u32[]{:S(2)}) %collective-permute-start.17) | collective-permute-done | bytes 131104 | tf_op jit(solution)/shard_map/errors_near/ppermute | solution.py:30
  68.0 1.3 %collective-permute-done.16.refs_1_ = f32[128,256]{1,0:T(8,128)S(1)} collective-permute-done((f32[128,256]{1,0:T(8,128)S(1)}, f32[128,256]{1,0:T(8,128)S(1)}, u32[]{:S(2)}, u32[]{:S(2)}) %collective-permute-start.16) | collective-permute-done | bytes 131104 | tf_op jit(solution)/shard_map/errors_near/ppermute | solution.py:30
  69.8 1.1 %collective-permute-start.23 = (f32[3,64,256]{2,1,0:T(8,128)S(1)}, f32[3,64,256]{2,1,0:T(8,128)S(1)}, u32[]{:S(2)}, u32[]{:S(2)}) collective-permute-start(f32[3,64,256]{2,1,0:T(8,128)S(1)} %pad_maximum_fusion.1), channel_id=1, source_target_pairs={{0,16},{1,17},{2,18},{3,19},{4,20},{5,21},{6,22},{7,23},{8,24},{9,... | collective-permute-start | bytes 589832 | tf_op jit(solution)/shard_map/errors_far/ppermute | solution.py:30
  70.9 2.2 %collective-permute-start.22 = (f32[3,64,256]{2,1,0:T(8,128)S(1)}, f32[3,64,256]{2,1,0:T(8,128)S(1)}, u32[]{:S(2)}, u32[]{:S(2)}) collective-permute-start(f32[3,64,256]{2,1,0:T(8,128)S(1)} %pad_maximum_fusion.1), channel_id=1, source_target_pairs={{0,8},{1,9},{2,10},{3,11},{4,12},{5,13},{6,14},{7,15},{8,16},{9,17... | collective-permute-start | bytes 589832 | tf_op jit(solution)/shard_map/errors_far/ppermute | solution.py:30
  73.8 0.9 collective-permute-start.26
  74.7 3.7 %collective-permute-done.24.refs_2_ = f32[3,64,256]{2,1,0:T(8,128)S(1)} collective-permute-done((f32[3,64,256]{2,1,0:T(8,128)S(1)}, f32[3,64,256]{2,1,0:T(8,128)S(1)}, u32[]{:S(2)}, u32[]{:S(2)}) %collective-permute-start.24) | collective-permute-done | bytes 196640 | tf_op jit(solution)/shard_map/errors_far/ppermute | solution.py:30
  78.4 0.8 layout.1.spread_ref
  79.1 4.4 %update.2.refs_6_ = f32[8192,128]{1,0:T(8,128)} custom-call(s32[5]{0:T(128)S(1)} %stack.63.place_ref, f32[8192,128]{1,0:T(8,128)} %bitcast.48, bf16[1536,512]{1,0:T(8,128)(2,1)S(1)} %layout.1.spread_ref, s32[16,4,128]{2,1,0:T(4,128)S(1)} %fusion.6.target_ref, f32[128,256]{1,0:T(8,128)S(1)} %broadcast_select_fusion.refs_0_, ...), custom_call_target="tpu_custom_call" | custom-call | flops 1879048192 | bytes 3670016 | tf_op jit(solution)/shard_map/update/pallas_call | solution.py:235
  83.5 1.7 %collective-permute-done.25.refs_3_ = f32[3,64,256]{2,1,0:T(8,128)S(1)} collective-permute-done((f32[3,64,256]{2,1,0:T(8,128)S(1)}, f32[3,64,256]{2,1,0:T(8,128)S(1)}, u32[]{:S(2)}, u32[]{:S(2)}) %collective-permute-start.25) | collective-permute-done | bytes 196640 | tf_op jit(solution)/shard_map/errors_far/ppermute | solution.py:30
  85.3 5.0 %update.3 = f32[8192,128]{1,0:T(8,128)} custom-call(s32[5]{0:T(128)S(1)} %stack.63.place_ref, f32[8192,128]{1,0:T(8,128)} %bitcast.49, bf16[1536,512]{1,0:T(8,128)(2,1)S(1)} %layout.1.spread_ref, s32[16,4,128]{2,1,0:T(4,128)S(1)} %fusion.6.target_ref, f32[3,64,256]{2,1,0:T(8,128)S(1)} %collective-permute-done.22.refs_0_, ...), custom_call_target="tpu_custom_call", output_to_operand_aliasing={{}: (10, {})} | custom-call | flops 2415919104 | bytes 4718592 | tf_op jit(solution)/shard_map/update/pallas_call | solution.py:235
  (54 shorter events, 6.2 us)
Async XLA Ops:
  0.0 6.8 %copy-start.1 = (f32[4,16,4,128]{3,2,1,0:T(4,128)S(1)}, f32[4,16,4,128]{3,2,1,0:T(4,128)}, u32[]{:S(2)}) copy-start(f32[4,16,4,128]{3,2,1,0:T(4,128)} %param.4) | copy-start | bytes 393220
  0.0 6.7 %collective-permute-start = (f32[256,128]{1,0:T(8,128)}, f32[256,128]{1,0:T(8,128)S(1)}, u32[]{:S(2)}, u32[]{:S(2)}) collective-permute-start(f32[256,128]{1,0:T(8,128)} %bitcast.53), channel_id=1, source_target_pairs={{0,64},{1,65},{2,66},{3,67},{4,68},{5,69},{6,70},{7,71},{8,72},{9,... | collective-permute-start | bytes 393224 | tf_op jit(solution)/shard_map/triangle_rows/ppermute | solution.py:30
  2.8 2.2 %copy-start = (f32[2048,4,128]{2,1,0:T(4,128)S(1)}, f32[2048,4,128]{2,1,0:T(4,128)}, u32[]{:S(2)}) copy-start(f32[2048,4,128]{2,1,0:T(4,128)} %param.3) | copy-start | bytes 12582916
  6.8 0.7 collective-permute-start.1
  7.6 3.4 %collective-permute-start.4 = (f32[256,128]{1,0:T(8,128)S(1)}, f32[256,128]{1,0:T(8,128)S(1)}, u32[]{:S(2)}, u32[]{:S(2)}) collective-permute-start(f32[256,128]{1,0:T(8,128)S(1)} %bitcast.58), channel_id=1, source_target_pairs={{0,24},{1,25},{2,26},{3,27},{32,56},{33,57},{34,58},{35,59},{64,88... | collective-permute-start | bytes 393224 | tf_op jit(solution)/shard_map/triangle_x/ppermute | solution.py:30
  8.2 3.4 %collective-permute-start.3 = (f32[256,128]{1,0:T(8,128)S(1)}, f32[256,128]{1,0:T(8,128)S(1)}, u32[]{:S(2)}, u32[]{:S(2)}) collective-permute-start(f32[256,128]{1,0:T(8,128)S(1)} %bitcast.59), channel_id=1, source_target_pairs={{0,16},{1,17},{2,18},{3,19},{32,48},{33,49},{34,50},{35,51},{64,80... | collective-permute-start | bytes 393224 | tf_op jit(solution)/shard_map/triangle_x/ppermute | solution.py:30
  8.9 4.3 %collective-permute-start.2 = (f32[256,128]{1,0:T(8,128)S(1)}, f32[256,128]{1,0:T(8,128)S(1)}, u32[]{:S(2)}, u32[]{:S(2)}) collective-permute-start(f32[256,128]{1,0:T(8,128)S(1)} %bitcast.60), channel_id=1, source_target_pairs={{0,8},{1,9},{2,10},{3,11},{32,40},{33,41},{34,42},{35,43},{64,72},... | collective-permute-start | bytes 393224 | tf_op jit(solution)/shard_map/triangle_x/ppermute | solution.py:30
  9.6 3.7 %collective-permute-start.7 = (f32[4,64,128]{2,1,0:T(8,128)S(1)}, f32[4,64,128]{2,1,0:T(8,128)S(1)}, u32[]{:S(2)}, u32[]{:S(2)}) collective-permute-start(f32[4,64,128]{2,1,0:T(8,128)S(1)} %get-tuple-element.53), channel_id=1, source_target_pairs={{0,16},{1,17},{2,18},{3,19},{32,48},{33,49},{34,50},{35,51},{64,80... | collective-permute-start | bytes 393224 | tf_op jit(solution)/shard_map/slab_x/ppermute | solution.py:30
  10.3 3.1 %collective-permute-start.6 = (f32[4,64,128]{2,1,0:T(8,128)S(1)}, f32[4,64,128]{2,1,0:T(8,128)S(1)}, u32[]{:S(2)}, u32[]{:S(2)}) collective-permute-start(f32[4,64,128]{2,1,0:T(8,128)S(1)} %get-tuple-element.54), channel_id=1, source_target_pairs={{0,8},{1,9},{2,10},{3,11},{32,40},{33,41},{34,42},{35,43},{64,72},... | collective-permute-start | bytes 393224 | tf_op jit(solution)/shard_map/slab_x/ppermute | solution.py:30
  11.0 2.4 %collective-permute-start.8 = (f32[4,64,128]{2,1,0:T(8,128)S(1)}, f32[4,64,128]{2,1,0:T(8,128)S(1)}, u32[]{:S(2)}, u32[]{:S(2)}) collective-permute-start(f32[4,64,128]{2,1,0:T(8,128)S(1)} %get-tuple-element.55), channel_id=1, source_target_pairs={{0,24},{1,25},{2,26},{3,27},{32,56},{33,57},{34,58},{35,59},{64,88... | collective-permute-start | bytes 393224 | tf_op jit(solution)/shard_map/slab_x/ppermute | solution.py:30
  11.7 12.4 %collective-permute-start.12 = (f32[2,256,128]{2,1,0:T(8,128)S(1)}, f32[2,256,128]{2,1,0:T(8,128)S(1)}, u32[]{:S(2)}, u32[]{:S(2)}) collective-permute-start(f32[2,256,128]{2,1,0:T(8,128)S(1)} %pad_maximum_fusion.refs_0_), channel_id=1, source_target_pairs={{0,128},{1,129},{2,130},{3,131},{4,132},{5,133},{6,134},{7,135},{8... | collective-permute-start | bytes 786440 | tf_op jit(solution)/shard_map/factor_chips/ppermute | solution.py:30
  13.3 1.4 %collective-permute-start.5 = (f32[256,128]{1,0:T(8,128)S(1)}, f32[256,128]{1,0:T(8,128)S(1)}, u32[]{:S(2)}, u32[]{:S(2)}) collective-permute-start(f32[256,128]{1,0:T(8,128)S(1)} %add_select_fusion.tri_ref), channel_id=1, source_target_pairs={{0,32},{1,33},{2,34},{3,35},{4,36},{5,37},{6,38},{7,39},{8,40},{9,... | collective-permute-start | bytes 393224 | tf_op jit(solution)/shard_map/triangle_y/ppermute | solution.py:30
  15.9 8.2 %collective-permute-start.9 = (f32[64,640]{1,0:T(8,128)S(1)}, f32[64,640]{1,0:T(8,128)S(1)}, u32[]{:S(2)}, u32[]{:S(2)}) collective-permute-start(f32[64,640]{1,0:T(8,128)S(1)} %get-tuple-element.33), channel_id=1, source_target_pairs={{0,1},{1,2},{2,3},{3,0},{4,5},{5,6},{6,7},{7,4},{8,9},{9,10},{10,1... | collective-permute-start | bytes 491528 | tf_op jit(solution)/shard_map/triangle_y/ppermute | solution.py:30
  17.6 10.6 %collective-permute-start.10 = (f32[64,640]{1,0:T(8,128)S(1)}, f32[64,640]{1,0:T(8,128)S(1)}, u32[]{:S(2)}, u32[]{:S(2)}) collective-permute-start(f32[64,640]{1,0:T(8,128)S(1)} %get-tuple-element.34), channel_id=1, source_target_pairs={{0,2},{1,3},{2,0},{3,1},{4,6},{5,7},{6,4},{7,5},{8,10},{9,11},{10,... | collective-permute-start | bytes 491528 | tf_op jit(solution)/shard_map/triangle_y/ppermute | solution.py:30
  20.5 7.7 %collective-permute-start.11 = (f32[64,640]{1,0:T(8,128)S(1)}, f32[64,640]{1,0:T(8,128)S(1)}, u32[]{:S(2)}, u32[]{:S(2)}) collective-permute-start(f32[64,640]{1,0:T(8,128)S(1)} %get-tuple-element.35), channel_id=1, source_target_pairs={{0,3},{1,0},{2,1},{3,2},{4,7},{5,4},{6,5},{7,6},{8,11},{9,8},{10,9... | collective-permute-start | bytes 491528 | tf_op jit(solution)/shard_map/triangle_y/ppermute | solution.py:30
  28.2 6.4 %collective-permute-start.13 = (f32[2,256,128]{2,1,0:T(8,128)S(1)}, f32[2,256,128]{2,1,0:T(8,128)S(1)}, u32[]{:S(2)}, u32[]{:S(2)}) collective-permute-start(f32[2,256,128]{2,1,0:T(8,128)S(1)} %pad_maximum_fusion.refs_0_), channel_id=1, source_target_pairs={{0,32},{1,33},{2,34},{3,35},{4,36},{5,37},{6,38},{7,39},{8,40},{9,... | collective-permute-start | bytes 786440 | tf_op jit(solution)/shard_map/factor_core/ppermute | solution.py:30
  28.2 6.4 %collective-permute-start.14 = (f32[2,256,128]{2,1,0:T(8,128)S(1)}, f32[2,256,128]{2,1,0:T(8,128)S(1)}, u32[]{:S(2)}, u32[]{:S(2)}) collective-permute-start(f32[2,256,128]{2,1,0:T(8,128)S(1)} %collective-permute-done.12.refs_1_), channel_id=1, source_target_pairs={{0,32},{1,33},{2,34},{3,35},{4,36},{5,37},{6,38},{7,39},{8,40},{9,... | collective-permute-start | bytes 786440 | tf_op jit(solution)/shard_map/factor_core/ppermute | solution.py:30
  34.7 18.8 %collective-permute-start.15 = (f32[128,256]{1,0:T(8,128)S(1)}, f32[128,256]{1,0:T(8,128)S(1)}, u32[]{:S(2)}, u32[]{:S(2)}) collective-permute-start(f32[128,256]{1,0:T(8,128)S(1)} %solve.1), channel_id=1, source_target_pairs={{0,4},{1,5},{2,6},{3,7},{8,12},{9,13},{10,14},{11,15},{16,20},{17,... | collective-permute-start | bytes 393224 | tf_op jit(solution)/shard_map/errors_plane/ppermute | solution.py:30
  53.5 8.2 %collective-permute-start.18 = (f32[128,256]{1,0:T(8,128)S(1)}, f32[128,256]{1,0:T(8,128)S(1)}, u32[]{:S(2)}, u32[]{:S(2)}) collective-permute-start(f32[128,256]{1,0:T(8,128)S(1)} %broadcast_select_fusion.refs_0_), channel_id=1, source_target_pairs={{0,3},{1,0},{2,1},{3,2},{4,7},{5,4},{6,5},{7,6},{8,11},{9,8},{10,9... | collective-permute-start | bytes 393224 | tf_op jit(solution)/shard_map/errors_near/ppermute | solution.py:30
  56.1 14.7 %collective-permute-start.21 = (f32[128,256]{1,0:T(8,128)S(1)}, f32[128,256]{1,0:T(8,128)S(1)}, u32[]{:S(2)}, u32[]{:S(2)}) collective-permute-start(f32[128,256]{1,0:T(8,128)S(1)} %broadcast_select_fusion.refs_0_), channel_id=1, source_target_pairs={{0,24},{1,25},{2,26},{3,27},{4,28},{5,29},{6,30},{7,31},{8,0},{9,1... | collective-permute-start | bytes 393224 | tf_op jit(solution)/shard_map/errors_near/ppermute | solution.py:30
  56.4 16.7 %collective-permute-start.20 = (f32[128,256]{1,0:T(8,128)S(1)}, f32[128,256]{1,0:T(8,128)S(1)}, u32[]{:S(2)}, u32[]{:S(2)}) collective-permute-start(f32[128,256]{1,0:T(8,128)S(1)} %broadcast_select_fusion.refs_0_), channel_id=1, source_target_pairs={{0,16},{1,17},{2,18},{3,19},{4,20},{5,21},{6,22},{7,23},{8,24},{9,... | collective-permute-start | bytes 393224 | tf_op jit(solution)/shard_map/errors_near/ppermute | solution.py:30
  59.6 13.6 %collective-permute-start.19 = (f32[128,256]{1,0:T(8,128)S(1)}, f32[128,256]{1,0:T(8,128)S(1)}, u32[]{:S(2)}, u32[]{:S(2)}) collective-permute-start(f32[128,256]{1,0:T(8,128)S(1)} %broadcast_select_fusion.refs_0_), channel_id=1, source_target_pairs={{0,8},{1,9},{2,10},{3,11},{4,12},{5,13},{6,14},{7,15},{8,16},{9,17... | collective-permute-start | bytes 393224 | tf_op jit(solution)/shard_map/errors_near/ppermute | solution.py:30
  61.4 6.6 %collective-permute-start.17 = (f32[128,256]{1,0:T(8,128)S(1)}, f32[128,256]{1,0:T(8,128)S(1)}, u32[]{:S(2)}, u32[]{:S(2)}) collective-permute-start(f32[128,256]{1,0:T(8,128)S(1)} %broadcast_select_fusion.refs_0_), channel_id=1, source_target_pairs={{0,2},{1,3},{2,0},{3,1},{4,6},{5,7},{6,4},{7,5},{8,10},{9,11},{10,... | collective-permute-start | bytes 393224 | tf_op jit(solution)/shard_map/errors_near/ppermute | solution.py:30
  61.7 7.5 %collective-permute-start.16 = (f32[128,256]{1,0:T(8,128)S(1)}, f32[128,256]{1,0:T(8,128)S(1)}, u32[]{:S(2)}, u32[]{:S(2)}) collective-permute-start(f32[128,256]{1,0:T(8,128)S(1)} %broadcast_select_fusion.refs_0_), channel_id=1, source_target_pairs={{0,1},{1,2},{2,3},{3,0},{4,5},{5,6},{6,7},{7,4},{8,9},{9,10},{10,1... | collective-permute-start | bytes 393224 | tf_op jit(solution)/shard_map/errors_near/ppermute | solution.py:30
  69.3 9.1 %collective-permute-start.24 = (f32[3,64,256]{2,1,0:T(8,128)S(1)}, f32[3,64,256]{2,1,0:T(8,128)S(1)}, u32[]{:S(2)}, u32[]{:S(2)}) collective-permute-start(f32[3,64,256]{2,1,0:T(8,128)S(1)} %pad_maximum_fusion.1), channel_id=1, source_target_pairs={{0,24},{1,25},{2,26},{3,27},{4,28},{5,29},{6,30},{7,31},{8,0},{9,1... | collective-permute-start | bytes 589832 | tf_op jit(solution)/shard_map/errors_far/ppermute | solution.py:30
  69.8 13.7 %collective-permute-start.23 = (f32[3,64,256]{2,1,0:T(8,128)S(1)}, f32[3,64,256]{2,1,0:T(8,128)S(1)}, u32[]{:S(2)}, u32[]{:S(2)}) collective-permute-start(f32[3,64,256]{2,1,0:T(8,128)S(1)} %pad_maximum_fusion.1), channel_id=1, source_target_pairs={{0,16},{1,17},{2,18},{3,19},{4,20},{5,21},{6,22},{7,23},{8,24},{9,... | collective-permute-start | bytes 589832 | tf_op jit(solution)/shard_map/errors_far/ppermute | solution.py:30
  70.9 12.7 %collective-permute-start.22 = (f32[3,64,256]{2,1,0:T(8,128)S(1)}, f32[3,64,256]{2,1,0:T(8,128)S(1)}, u32[]{:S(2)}, u32[]{:S(2)}) collective-permute-start(f32[3,64,256]{2,1,0:T(8,128)S(1)} %pad_maximum_fusion.1), channel_id=1, source_target_pairs={{0,8},{1,9},{2,10},{3,11},{4,12},{5,13},{6,14},{7,15},{8,16},{9,17... | collective-permute-start | bytes 589832 | tf_op jit(solution)/shard_map/errors_far/ppermute | solution.py:30
  73.2 10.3 %collective-permute-start.27 = (f32[3,64,256]{2,1,0:T(8,128)S(1)}, f32[3,64,256]{2,1,0:T(8,128)S(1)}, u32[]{:S(2)}, u32[]{:S(2)}) collective-permute-start(f32[3,64,256]{2,1,0:T(8,128)S(1)} %pad_maximum_fusion.2), channel_id=1, source_target_pairs={{0,3},{1,0},{2,1},{3,2},{4,7},{5,4},{6,5},{7,6},{8,11},{9,8},{10,9... | collective-permute-start | bytes 589832 | tf_op jit(solution)/shard_map/errors_far/ppermute | solution.py:30
  73.8 9.7 %collective-permute-start.26 = (f32[3,64,256]{2,1,0:T(8,128)S(1)}, f32[3,64,256]{2,1,0:T(8,128)S(1)}, u32[]{:S(2)}, u32[]{:S(2)}) collective-permute-start(f32[3,64,256]{2,1,0:T(8,128)S(1)} %pad_maximum_fusion.2), channel_id=1, source_target_pairs={{0,2},{1,3},{2,0},{3,1},{4,6},{5,7},{6,4},{7,5},{8,10},{9,11},{10,... | collective-permute-start | bytes 589832 | tf_op jit(solution)/shard_map/errors_far/ppermute | solution.py:30
  78.4 6.9 %collective-permute-start.25 = (f32[3,64,256]{2,1,0:T(8,128)S(1)}, f32[3,64,256]{2,1,0:T(8,128)S(1)}, u32[]{:S(2)}, u32[]{:S(2)}) collective-permute-start(f32[3,64,256]{2,1,0:T(8,128)S(1)} %pad_maximum_fusion.2), channel_id=1, source_target_pairs={{0,1},{1,2},{2,3},{3,0},{4,5},{5,6},{6,7},{7,4},{8,9},{9,10},{10,1... | collective-permute-start | bytes 589832 | tf_op jit(solution)/shard_map/errors_far/ppermute | solution.py:30

commit v4 on v3

--- a/solution.py
+++ b/solution.py
@@ -184,11 +184,8 @@
             pick = pick_ref[...]
             here = slice((k - start) * BW, (k - start + 1) * BW)
             what = plan[k]
-            if len(what) == 1:
-                value = errors[what[0]][...]
-            else:
-                (r0, i0), (r1, i1) = what
-                value = jnp.concatenate([errors[r0][i0], errors[r1][i1]], axis=0)
+            parts = [errors[ref][begin:end, :] for ref, begin, end in what]
+            value = parts[0] if len(parts) == 1 else jnp.concatenate(parts, axis=0)
             high, low = split(value)
             wide = NB * BW
             high = dot(high, pick).astype(BF16)
@@ -251,6 +248,17 @@
     )(*operands)
 
 
+def far_parts(s, t):
+    half = BW // 2
+    if s == 2 and t == 2:
+        return [(1, 0, half), (4, 0, half)]
+    if s == 2:
+        return [(t - 1, BW, 2 * BW)]
+    if t == 2:
+        return [(2 + s, BW, 2 * BW)]
+    return [(t - 1, (s // 2) * half, (s // 2 + 1) * half), (2 + s, (t // 2) * half, (t // 2 + 1) * half)]
+
+
 def local(weights, factor, keep_masks):
     me, row = lax.axis_index("col"), lax.axis_index("row")
     x, z, y = me >> 3, (me >> 2) & 1, me & 3
@@ -358,22 +366,22 @@
         )(place, *chips, *other_chips)
 
     with jax.named_scope("errors_far"):
-        top = jnp.stack([piece[:half] for piece in by_y])
-        bottom = jnp.stack([piece[half:] for piece in by_x])
-        top_x = [shift(top, t, 0) for t in (1, 2, 3)]
-        bottom_y = [shift(bottom, 0, s) for s in (1, 2, 3)]
+        top = jnp.concatenate([by_y[0][:half], by_y[2][:half], by_y[1]])
+        bottom = jnp.concatenate([by_x[0][half:], by_x[2][half:], by_x[1]])
+        top_x = [shift(top, 1, 0), shift(by_y[1][:half], 2, 0), shift(top, 3, 0)]
+        bottom_y = [shift(bottom, 0, 1), shift(by_x[1][half:], 0, 2), shift(bottom, 0, 3)]
 
     with jax.named_scope("update"):
         first = [(0, 0)] + [(s, 0) for s in (1, 2, 3)] + [(0, t) for t in (1, 2, 3)]
         out = update(
             place, flat, spread, target,
-            [errors, *by_y, *by_x], [(k,) for k in range(7)], first,
+            [errors, *by_y, *by_x], [[(k, 0, BW)] for k in range(7)], first,
         )
         out, top_x, bottom_y = barrier((out, top_x, bottom_y))
         second = [(s, t) for s in (1, 2, 3) for t in (1, 2, 3)]
         out = update(
             place, flat, spread, target,
-            [*top_x, *bottom_y], [((t - 1, s - 1), (3 + s - 1, t - 1)) for s, t in second], second, out,
+            [*top_x, *bottom_y], [far_parts(s, t) for s, t in second], second, out,
         )
     return out.reshape(weights.shape)
 

time: 92 us -> 91.6 us (level)
  the two profiles are of different devices: /device:TPU:198 before, /device:TPU:160 now
where the time goes in v4:
time: 91.6 us; the launch traced here: 91.1 us
  waiting for transfers between devices  34.5 us (38%)
  starting transfers between devices  32.9 us (36%)
  Pallas kernels  18.9 us (21%)
  local copies, waits for them, and re-layouts  2.35 us (3%)
  other arithmetic  1.82 us (2%)
    ppermute x28, waiting for transfers between devices, permute(): return lax.ppermute(value, ('row', 'col'), pairs)  34.5 us
    ppermute x28, starting transfers between devices, permute(): return lax.ppermute(value, ('row', 'col'), pairs)  32.9 us
    pallas_call x2, Pallas kernels, update(): pl.pallas_call(functools.partial(update_kernel, pieces=(errors, plan, pla...  9.34 us
    pallas_call x1, Pallas kernels, local(): pl.pallas_call(solve_kernel, out_shape=jax.ShapeDtypeStruct((BW, KACT), F...  5.91 us
    unnamed x4, local copies, waits for them, and re-layouts  2.21 us
  transfers between devices with their start and end apart: 28, of which 6 were waited for; matrix products, arithmetic and copies ran while one was open for 2% of the time, Pallas kernels for 15%

profile of v4, /device:TPU:160, one launch (start us, length us, event | category | flops | bytes accessed | tf_op | source)
XLA Modules:
  0.0 91.1 jit_solution(1330536606307397621)
XLA Ops:
  0.0 1.0 %collective-permute-start = (f32[256,128]{1,0:T(8,128)}, f32[256,128]{1,0:T(8,128)S(1)}, u32[]{:S(2)}, u32[]{:S(2)}) collective-permute-start(f32[256,128]{1,0:T(8,128)} %bitcast.41), channel_id=1, source_target_pairs={{0,64},{1,65},{2,66},{3,67},{4,68},{5,69},{6,70},{7,71},{8,72},{9,... | collective-permute-start | bytes 393224 | tf_op jit(solution)/shard_map/triangle_rows/ppermute | solution.py:30
  1.0 0.8 subtract_convert_fusion
  1.9 0.8 fusion.6.target_ref
  2.8 2.2 %copy-done = f32[2048,4,128]{2,1,0:T(4,128)S(1)} copy-done((f32[2048,4,128]{2,1,0:T(4,128)S(1)}, f32[2048,4,128]{2,1,0:T(4,128)}, u32[]{:S(2)}) %copy-start) | copy-done | bytes 4194328
  5.0 1.7 %compact.1 = f32[16,64,128]{2,1,0:T(8,128)S(1)} custom-call(s32[5]{0:T(128)S(1)} %stack.39.place_ref, f32[8192,128]{1,0:T(8,128)S(1)} %bitcast.38, s32[16,4,128]{2,1,0:T(4,128)S(1)} %fusion.6.target_ref), custom_call_target="tpu_custom_call" | custom-call | flops 1073741824 | bytes 16777216 | tf_op jit(solution)/shard_map/compact/pallas_call | solution.py:283
  8.2 0.7 collective-permute-start.3
  8.9 0.7 collective-permute-start.2
  11.0 0.7 collective-permute-start.8
  11.7 1.6 %collective-permute-start.12 = (f32[2,256,128]{2,1,0:T(8,128)S(1)}, f32[2,256,128]{2,1,0:T(8,128)S(1)}, u32[]{:S(2)}, u32[]{:S(2)}) collective-permute-start(f32[2,256,128]{2,1,0:T(8,128)S(1)} %pad_maximum_fusion.refs_0_), channel_id=1, source_target_pairs={{0,128},{1,129},{2,130},{3,131},{4,132},{5,133},{6,134},{7,135},{8... | collective-permute-start | bytes 786440 | tf_op jit(solution)/shard_map/factor_chips/ppermute | solution.py:30
  13.4 1.3 %collective-permute-done.5.other_ref = f32[256,128]{1,0:T(8,128)S(1)} collective-permute-done((f32[256,128]{1,0:T(8,128)S(1)}, f32[256,128]{1,0:T(8,128)S(1)}, u32[]{:S(2)}, u32[]{:S(2)}) %collective-permute-start.5) | collective-permute-done | bytes 131104 | tf_op jit(solution)/shard_map/triangle_y/ppermute | solution.py:30
  14.7 1.2 %triangle_y.1 = (f32[64,640]{1,0:T(8,128)S(1)}, f32[64,640]{1,0:T(8,128)S(1)}, f32[64,640]{1,0:T(8,128)S(1)}, f32[64,640]{1,0:T(8,128)S(1)}) custom-call(s32[5]{0:T(128)S(1)} %stack.39.place_ref, f32[256,128]{1,0:T(8,128)S(1)} %add_select_fusion.tri_ref, f32[256,128]{1,0:T(8,128)S(1)} %collective-permute-done.5.other_ref, f32[4,64,128]{2,1,0:T(8,128)S(1)} %fusion.slabs_ref, ...), custom_call_target="tpu_custom_call" | custom-call | flops 268435456 | bytes 1048576 | tf_op jit(solution)/shard_map/triangle_y/pallas_call | solution.py:315
  15.9 1.7 %collective-permute-start.9 = (f32[64,640]{1,0:T(8,128)S(1)}, f32[64,640]{1,0:T(8,128)S(1)}, u32[]{:S(2)}, u32[]{:S(2)}) collective-permute-start(f32[64,640]{1,0:T(8,128)S(1)} %get-tuple-element.33), channel_id=1, source_target_pairs={{0,1},{1,2},{2,3},{3,0},{4,5},{5,6},{6,7},{7,4},{8,9},{9,10},{10,1... | collective-permute-start | bytes 491528 | tf_op jit(solution)/shard_map/triangle_y/ppermute | solution.py:30
  17.6 2.9 %collective-permute-start.10 = (f32[64,640]{1,0:T(8,128)S(1)}, f32[64,640]{1,0:T(8,128)S(1)}, u32[]{:S(2)}, u32[]{:S(2)}) collective-permute-start(f32[64,640]{1,0:T(8,128)S(1)} %get-tuple-element.34), channel_id=1, source_target_pairs={{0,2},{1,3},{2,0},{3,1},{4,6},{5,7},{6,4},{7,5},{8,10},{9,11},{10,... | collective-permute-start | bytes 491528 | tf_op jit(solution)/shard_map/triangle_y/ppermute | solution.py:30
  20.5 1.3 %collective-permute-start.11 = (f32[64,640]{1,0:T(8,128)S(1)}, f32[64,640]{1,0:T(8,128)S(1)}, u32[]{:S(2)}, u32[]{:S(2)}) collective-permute-start(f32[64,640]{1,0:T(8,128)S(1)} %get-tuple-element.35), channel_id=1, source_target_pairs={{0,3},{1,0},{2,1},{3,2},{4,7},{5,4},{6,5},{7,6},{8,11},{9,8},{10,9... | collective-permute-start | bytes 491528 | tf_op jit(solution)/shard_map/triangle_y/ppermute | solution.py:30
  21.8 2.3 %collective-permute-done.12.refs_1_ = f32[2,256,128]{2,1,0:T(8,128)S(1)} collective-permute-done((f32[2,256,128]{2,1,0:T(8,128)S(1)}, f32[2,256,128]{2,1,0:T(8,128)S(1)}, u32[]{:S(2)}, u32[]{:S(2)}) %collective-permute-start.12) | collective-permute-done | bytes 262176 | tf_op jit(solution)/shard_map/factor_chips/ppermute | solution.py:30
  24.1 4.1 %collective-permute-done.10.p2 = f32[64,640]{1,0:T(8,128)S(1)} collective-permute-done((f32[64,640]{1,0:T(8,128)S(1)}, f32[64,640]{1,0:T(8,128)S(1)}, u32[]{:S(2)}, u32[]{:S(2)}) %collective-permute-start.10) | collective-permute-done | bytes 163872 | tf_op jit(solution)/shard_map/triangle_y/ppermute | solution.py:30
  28.8 5.9 %solve.1 = f32[128,256]{1,0:T(8,128)S(1)} custom-call(s32[5]{0:T(128)S(1)} %stack.39.place_ref, f32[64,640]{1,0:T(8,128)S(1)} %get-tuple-element.39.p0, f32[64,640]{1,0:T(8,128)S(1)} %collective-permute-done.9.p1, f32[64,640]{1,0:T(8,128)S(1)} %collective-permute-done.10.p2, f32[64,640]{1,0:T(8,128)S(1)} %collective-permute-done.11.p3, ...), custom_call_target="tpu_custom_call" | custom-call | flops 2147483648 | bytes 2097152 | tf_op jit(solution)/shard_map/solve/pallas_call | solution.py:334
  34.7 1.3 %collective-permute-start.15 = (f32[128,256]{1,0:T(8,128)S(1)}, f32[128,256]{1,0:T(8,128)S(1)}, u32[]{:S(2)}, u32[]{:S(2)}) collective-permute-start(f32[128,256]{1,0:T(8,128)S(1)} %solve.1), channel_id=1, source_target_pairs={{0,4},{1,5},{2,6},{3,7},{8,12},{9,13},{10,14},{11,15},{16,20},{17,... | collective-permute-start | bytes 393224 | tf_op jit(solution)/shard_map/errors_plane/ppermute | solution.py:30
  36.0 18.8 %collective-permute-done.15 = f32[128,256]{1,0:T(8,128)S(1)} collective-permute-done((f32[128,256]{1,0:T(8,128)S(1)}, f32[128,256]{1,0:T(8,128)S(1)}, u32[]{:S(2)}, u32[]{:S(2)}) %collective-permute-start.15) | collective-permute-done | bytes 131104 | tf_op jit(solution)/shard_map/errors_plane/ppermute | solution.py:30
  54.8 2.7 %collective-permute-start.18 = (f32[128,256]{1,0:T(8,128)S(1)}, f32[128,256]{1,0:T(8,128)S(1)}, u32[]{:S(2)}, u32[]{:S(2)}) collective-permute-start(f32[128,256]{1,0:T(8,128)S(1)} %broadcast_select_fusion.refs_0_), channel_id=1, source_target_pairs={{0,3},{1,0},{2,1},{3,2},{4,7},{5,4},{6,5},{7,6},{8,11},{9,8},{10,9... | collective-permute-start | bytes 393224 | tf_op jit(solution)/shard_map/errors_near/ppermute | solution.py:30
  57.5 1.9 %collective-permute-start.17 = (f32[128,256]{1,0:T(8,128)S(1)}, f32[128,256]{1,0:T(8,128)S(1)}, u32[]{:S(2)}, u32[]{:S(2)}) collective-permute-start(f32[128,256]{1,0:T(8,128)S(1)} %broadcast_select_fusion.refs_0_), channel_id=1, source_target_pairs={{0,2},{1,3},{2,0},{3,1},{4,6},{5,7},{6,4},{7,5},{8,10},{9,11},{10,... | collective-permute-start | bytes 393224 | tf_op jit(solution)/shard_map/errors_near/ppermute | solution.py:30
  59.4 2.0 %collective-permute-start.19 = (f32[128,256]{1,0:T(8,128)S(1)}, f32[128,256]{1,0:T(8,128)S(1)}, u32[]{:S(2)}, u32[]{:S(2)}) collective-permute-start(f32[128,256]{1,0:T(8,128)S(1)} %broadcast_select_fusion.refs_0_), channel_id=1, source_target_pairs={{0,8},{1,9},{2,10},{3,11},{4,12},{5,13},{6,14},{7,15},{8,16},{9,17... | collective-permute-start | bytes 393224 | tf_op jit(solution)/shard_map/errors_near/ppermute | solution.py:30
  61.4 1.5 %collective-permute-start.20 = (f32[128,256]{1,0:T(8,128)S(1)}, f32[128,256]{1,0:T(8,128)S(1)}, u32[]{:S(2)}, u32[]{:S(2)}) collective-permute-start(f32[128,256]{1,0:T(8,128)S(1)} %broadcast_select_fusion.refs_0_), channel_id=1, source_target_pairs={{0,16},{1,17},{2,18},{3,19},{4,20},{5,21},{6,22},{7,23},{8,24},{9,... | collective-permute-start | bytes 393224 | tf_op jit(solution)/shard_map/errors_near/ppermute | solution.py:30
  62.9 3.7 %collective-permute-done.16.refs_1_ = f32[128,256]{1,0:T(8,128)S(1)} collective-permute-done((f32[128,256]{1,0:T(8,128)S(1)}, f32[128,256]{1,0:T(8,128)S(1)}, u32[]{:S(2)}, u32[]{:S(2)}) %collective-permute-start.16) | collective-permute-done | bytes 131104 | tf_op jit(solution)/shard_map/errors_near/ppermute | solution.py:30
  66.7 2.0 %collective-permute-start.22 = (f32[256,256]{1,0:T(8,128)S(1)}, f32[256,256]{1,0:T(8,128)S(1)}, u32[]{:S(2)}, u32[]{:S(2)}) collective-permute-start(f32[256,256]{1,0:T(8,128)S(1)} %pad_maximum_fusion.1), channel_id=1, source_target_pairs={{0,8},{1,9},{2,10},{3,11},{4,12},{5,13},{6,14},{7,15},{8,16},{9,17... | collective-permute-start | bytes 786440 | tf_op jit(solution)/shard_map/errors_far/ppermute | solution.py:30
  68.8 3.2 %collective-permute-start.27 = (f32[256,256]{1,0:T(8,128)S(1)}, f32[256,256]{1,0:T(8,128)S(1)}, u32[]{:S(2)}, u32[]{:S(2)}) collective-permute-start(f32[256,256]{1,0:T(8,128)S(1)} %pad_maximum_fusion.2), channel_id=1, source_target_pairs={{0,3},{1,0},{2,1},{3,2},{4,7},{5,4},{6,5},{7,6},{8,11},{9,8},{10,9... | collective-permute-start | bytes 786440 | tf_op jit(solution)/shard_map/errors_far/ppermute | solution.py:30
  72.1 1.9 %collective-permute-start.26 = (f32[64,256]{1,0:T(8,128)S(1)}, f32[64,256]{1,0:T(8,128)S(1)}, u32[]{:S(2)}, u32[]{:S(2)}) collective-permute-start(f32[64,256]{1,0:T(8,128)S(1)} %slice.53), channel_id=1, source_target_pairs={{0,2},{1,3},{2,0},{3,1},{4,6},{5,7},{6,4},{7,5},{8,10},{9,11},{10,... | collective-permute-start | bytes 196616 | tf_op jit(solution)/shard_map/errors_far/ppermute | solution.py:30
  74.0 0.7 layout.1.spread_ref
  74.8 4.3 %collective-permute-done.26.refs_4_ = f32[64,256]{1,0:T(8,128)S(1)} collective-permute-done((f32[64,256]{1,0:T(8,128)S(1)}, f32[64,256]{1,0:T(8,128)S(1)}, u32[]{:S(2)}, u32[]{:S(2)}) %collective-permute-start.26) | collective-permute-done | bytes 65568 | tf_op jit(solution)/shard_map/errors_far/ppermute | solution.py:30
  79.1 2.5 %collective-permute-start.23 = (f32[64,256]{1,0:T(8,128)S(1)}, f32[64,256]{1,0:T(8,128)S(1)}, u32[]{:S(2)}, u32[]{:S(2)}) collective-permute-start(f32[64,256]{1,0:T(8,128)S(1)} %slice.50), channel_id=1, source_target_pairs={{0,16},{1,17},{2,18},{3,19},{4,20},{5,21},{6,22},{7,23},{8,24},{9,... | collective-permute-start | bytes 196616 | tf_op jit(solution)/shard_map/errors_far/ppermute | solution.py:30
  81.6 4.4 %update.2.refs_6_ = f32[8192,128]{1,0:T(8,128)} custom-call(s32[5]{0:T(128)S(1)} %stack.39.place_ref, f32[8192,128]{1,0:T(8,128)} %bitcast.36, bf16[1536,512]{1,0:T(8,128)(2,1)S(1)} %layout.1.spread_ref, s32[16,4,128]{2,1,0:T(4,128)S(1)} %fusion.6.target_ref, f32[128,256]{1,0:T(8,128)S(1)} %broadcast_select_fusion.refs_0_, ...), custom_call_target="tpu_custom_call" | custom-call | flops 1879048192 | bytes 3670016 | tf_op jit(solution)/shard_map/update/pallas_call | solution.py:232
  86.0 5.0 %update.3 = f32[8192,128]{1,0:T(8,128)} custom-call(s32[5]{0:T(128)S(1)} %stack.39.place_ref, f32[8192,128]{1,0:T(8,128)} %bitcast.37, bf16[1536,512]{1,0:T(8,128)(2,1)S(1)} %layout.1.spread_ref, s32[16,4,128]{2,1,0:T(4,128)S(1)} %fusion.6.target_ref, f32[256,256]{1,0:T(8,128)S(1)} %collective-permute-done.22.refs_0_, ...), custom_call_target="tpu_custom_call", output_to_operand_aliasing={{}: (10, {})} | custom-call | flops 2415919104 | bytes 4718592 | tf_op jit(solution)/shard_map/update/pallas_call | solution.py:232
  (54 shorter events, 3.9 us)
Async XLA Ops:
  0.0 6.7 %copy-start.1 = (f32[4,16,4,128]{3,2,1,0:T(4,128)S(1)}, f32[4,16,4,128]{3,2,1,0:T(4,128)}, u32[]{:S(2)}) copy-start(f32[4,16,4,128]{3,2,1,0:T(4,128)} %param.4) | copy-start | bytes 393220
  0.0 6.7 %collective-permute-start = (f32[256,128]{1,0:T(8,128)}, f32[256,128]{1,0:T(8,128)S(1)}, u32[]{:S(2)}, u32[]{:S(2)}) collective-permute-start(f32[256,128]{1,0:T(8,128)} %bitcast.41), channel_id=1, source_target_pairs={{0,64},{1,65},{2,66},{3,67},{4,68},{5,69},{6,70},{7,71},{8,72},{9,... | collective-permute-start | bytes 393224 | tf_op jit(solution)/shard_map/triangle_rows/ppermute | solution.py:30
  2.8 2.2 %copy-start = (f32[2048,4,128]{2,1,0:T(4,128)S(1)}, f32[2048,4,128]{2,1,0:T(4,128)}, u32[]{:S(2)}) copy-start(f32[2048,4,128]{2,1,0:T(4,128)} %param.3) | copy-start | bytes 12582916
  6.8 0.7 collective-permute-start.1
  7.5 3.4 %collective-permute-start.4 = (f32[256,128]{1,0:T(8,128)S(1)}, f32[256,128]{1,0:T(8,128)S(1)}, u32[]{:S(2)}, u32[]{:S(2)}) collective-permute-start(f32[256,128]{1,0:T(8,128)S(1)} %bitcast.46), channel_id=1, source_target_pairs={{0,24},{1,25},{2,26},{3,27},{32,56},{33,57},{34,58},{35,59},{64,88... | collective-permute-start | bytes 393224 | tf_op jit(solution)/shard_map/triangle_x/ppermute | solution.py:30
  8.2 3.4 %collective-permute-start.3 = (f32[256,128]{1,0:T(8,128)S(1)}, f32[256,128]{1,0:T(8,128)S(1)}, u32[]{:S(2)}, u32[]{:S(2)}) collective-permute-start(f32[256,128]{1,0:T(8,128)S(1)} %bitcast.47), channel_id=1, source_target_pairs={{0,16},{1,17},{2,18},{3,19},{32,48},{33,49},{34,50},{35,51},{64,80... | collective-permute-start | bytes 393224 | tf_op jit(solution)/shard_map/triangle_x/ppermute | solution.py:30
  8.9 4.3 %collective-permute-start.2 = (f32[256,128]{1,0:T(8,128)S(1)}, f32[256,128]{1,0:T(8,128)S(1)}, u32[]{:S(2)}, u32[]{:S(2)}) collective-permute-start(f32[256,128]{1,0:T(8,128)S(1)} %bitcast.48), channel_id=1, source_target_pairs={{0,8},{1,9},{2,10},{3,11},{32,40},{33,41},{34,42},{35,43},{64,72},... | collective-permute-start | bytes 393224 | tf_op jit(solution)/shard_map/triangle_x/ppermute | solution.py:30
  9.6 3.7 %collective-permute-start.7 = (f32[4,64,128]{2,1,0:T(8,128)S(1)}, f32[4,64,128]{2,1,0:T(8,128)S(1)}, u32[]{:S(2)}, u32[]{:S(2)}) collective-permute-start(f32[4,64,128]{2,1,0:T(8,128)S(1)} %get-tuple-element.53), channel_id=1, source_target_pairs={{0,16},{1,17},{2,18},{3,19},{32,48},{33,49},{34,50},{35,51},{64,80... | collective-permute-start | bytes 393224 | tf_op jit(solution)/shard_map/slab_x/ppermute | solution.py:30
  10.3 3.1 %collective-permute-start.6 = (f32[4,64,128]{2,1,0:T(8,128)S(1)}, f32[4,64,128]{2,1,0:T(8,128)S(1)}, u32[]{:S(2)}, u32[]{:S(2)}) collective-permute-start(f32[4,64,128]{2,1,0:T(8,128)S(1)} %get-tuple-element.54), channel_id=1, source_target_pairs={{0,8},{1,9},{2,10},{3,11},{32,40},{33,41},{34,42},{35,43},{64,72},... | collective-permute-start | bytes 393224 | tf_op jit(solution)/shard_map/slab_x/ppermute | solution.py:30
  11.0 2.4 %collective-permute-start.8 = (f32[4,64,128]{2,1,0:T(8,128)S(1)}, f32[4,64,128]{2,1,0:T(8,128)S(1)}, u32[]{:S(2)}, u32[]{:S(2)}) collective-permute-start(f32[4,64,128]{2,1,0:T(8,128)S(1)} %get-tuple-element.55), channel_id=1, source_target_pairs={{0,24},{1,25},{2,26},{3,27},{32,56},{33,57},{34,58},{35,59},{64,88... | collective-permute-start | bytes 393224 | tf_op jit(solution)/shard_map/slab_x/ppermute | solution.py:30
  11.7 12.5 %collective-permute-start.12 = (f32[2,256,128]{2,1,0:T(8,128)S(1)}, f32[2,256,128]{2,1,0:T(8,128)S(1)}, u32[]{:S(2)}, u32[]{:S(2)}) collective-permute-start(f32[2,256,128]{2,1,0:T(8,128)S(1)} %pad_maximum_fusion.refs_0_), channel_id=1, source_target_pairs={{0,128},{1,129},{2,130},{3,131},{4,132},{5,133},{6,134},{7,135},{8... | collective-permute-start | bytes 786440 | tf_op jit(solution)/shard_map/factor_chips/ppermute | solution.py:30
  13.3 1.4 %collective-permute-start.5 = (f32[256,128]{1,0:T(8,128)S(1)}, f32[256,128]{1,0:T(8,128)S(1)}, u32[]{:S(2)}, u32[]{:S(2)}) collective-permute-start(f32[256,128]{1,0:T(8,128)S(1)} %add_select_fusion.tri_ref), channel_id=1, source_target_pairs={{0,32},{1,33},{2,34},{3,35},{4,36},{5,37},{6,38},{7,39},{8,40},{9,... | collective-permute-start | bytes 393224 | tf_op jit(solution)/shard_map/triangle_y/ppermute | solution.py:30
  15.9 8.2 %collective-permute-start.9 = (f32[64,640]{1,0:T(8,128)S(1)}, f32[64,640]{1,0:T(8,128)S(1)}, u32[]{:S(2)}, u32[]{:S(2)}) collective-permute-start(f32[64,640]{1,0:T(8,128)S(1)} %get-tuple-element.33), channel_id=1, source_target_pairs={{0,1},{1,2},{2,3},{3,0},{4,5},{5,6},{6,7},{7,4},{8,9},{9,10},{10,1... | collective-permute-start | bytes 491528 | tf_op jit(solution)/shard_map/triangle_y/ppermute | solution.py:30
  17.6 10.6 %collective-permute-start.10 = (f32[64,640]{1,0:T(8,128)S(1)}, f32[64,640]{1,0:T(8,128)S(1)}, u32[]{:S(2)}, u32[]{:S(2)}) collective-permute-start(f32[64,640]{1,0:T(8,128)S(1)} %get-tuple-element.34), channel_id=1, source_target_pairs={{0,2},{1,3},{2,0},{3,1},{4,6},{5,7},{6,4},{7,5},{8,10},{9,11},{10,... | collective-permute-start | bytes 491528 | tf_op jit(solution)/shard_map/triangle_y/ppermute | solution.py:30
  20.5 7.7 %collective-permute-start.11 = (f32[64,640]{1,0:T(8,128)S(1)}, f32[64,640]{1,0:T(8,128)S(1)}, u32[]{:S(2)}, u32[]{:S(2)}) collective-permute-start(f32[64,640]{1,0:T(8,128)S(1)} %get-tuple-element.35), channel_id=1, source_target_pairs={{0,3},{1,0},{2,1},{3,2},{4,7},{5,4},{6,5},{7,6},{8,11},{9,8},{10,9... | collective-permute-start | bytes 491528 | tf_op jit(solution)/shard_map/triangle_y/ppermute | solution.py:30
  28.2 6.4 %collective-permute-start.13 = (f32[2,256,128]{2,1,0:T(8,128)S(1)}, f32[2,256,128]{2,1,0:T(8,128)S(1)}, u32[]{:S(2)}, u32[]{:S(2)}) collective-permute-start(f32[2,256,128]{2,1,0:T(8,128)S(1)} %pad_maximum_fusion.refs_0_), channel_id=1, source_target_pairs={{0,32},{1,33},{2,34},{3,35},{4,36},{5,37},{6,38},{7,39},{8,40},{9,... | collective-permute-start | bytes 786440 | tf_op jit(solution)/shard_map/factor_core/ppermute | solution.py:30
  28.2 6.4 %collective-permute-start.14 = (f32[2,256,128]{2,1,0:T(8,128)S(1)}, f32[2,256,128]{2,1,0:T(8,128)S(1)}, u32[]{:S(2)}, u32[]{:S(2)}) collective-permute-start(f32[2,256,128]{2,1,0:T(8,128)S(1)} %collective-permute-done.12.refs_1_), channel_id=1, source_target_pairs={{0,32},{1,33},{2,34},{3,35},{4,36},{5,37},{6,38},{7,39},{8,40},{9,... | collective-permute-start | bytes 786440 | tf_op jit(solution)/shard_map/factor_core/ppermute | solution.py:30
  34.7 20.1 %collective-permute-start.15 = (f32[128,256]{1,0:T(8,128)S(1)}, f32[128,256]{1,0:T(8,128)S(1)}, u32[]{:S(2)}, u32[]{:S(2)}) collective-permute-start(f32[128,256]{1,0:T(8,128)S(1)} %solve.1), channel_id=1, source_target_pairs={{0,4},{1,5},{2,6},{3,7},{8,12},{9,13},{10,14},{11,15},{16,20},{17,... | collective-permute-start | bytes 393224 | tf_op jit(solution)/shard_map/errors_plane/ppermute | solution.py:30
  54.8 6.6 %collective-permute-start.18 = (f32[128,256]{1,0:T(8,128)S(1)}, f32[128,256]{1,0:T(8,128)S(1)}, u32[]{:S(2)}, u32[]{:S(2)}) collective-permute-start(f32[128,256]{1,0:T(8,128)S(1)} %broadcast_select_fusion.refs_0_), channel_id=1, source_target_pairs={{0,3},{1,0},{2,1},{3,2},{4,7},{5,4},{6,5},{7,6},{8,11},{9,8},{10,9... | collective-permute-start | bytes 393224 | tf_op jit(solution)/shard_map/errors_near/ppermute | solution.py:30
  57.5 9.1 %collective-permute-start.16 = (f32[128,256]{1,0:T(8,128)S(1)}, f32[128,256]{1,0:T(8,128)S(1)}, u32[]{:S(2)}, u32[]{:S(2)}) collective-permute-start(f32[128,256]{1,0:T(8,128)S(1)} %broadcast_select_fusion.refs_0_), channel_id=1, source_target_pairs={{0,1},{1,2},{2,3},{3,0},{4,5},{5,6},{6,7},{7,4},{8,9},{9,10},{10,1... | collective-permute-start | bytes 393224 | tf_op jit(solution)/shard_map/errors_near/ppermute | solution.py:30
  57.5 9.1 %collective-permute-start.17 = (f32[128,256]{1,0:T(8,128)S(1)}, f32[128,256]{1,0:T(8,128)S(1)}, u32[]{:S(2)}, u32[]{:S(2)}) collective-permute-start(f32[128,256]{1,0:T(8,128)S(1)} %broadcast_select_fusion.refs_0_), channel_id=1, source_target_pairs={{0,2},{1,3},{2,0},{3,1},{4,6},{5,7},{6,4},{7,5},{8,10},{9,11},{10,... | collective-permute-start | bytes 393224 | tf_op jit(solution)/shard_map/errors_near/ppermute | solution.py:30
  59.4 9.4 %collective-permute-start.21 = (f32[128,256]{1,0:T(8,128)S(1)}, f32[128,256]{1,0:T(8,128)S(1)}, u32[]{:S(2)}, u32[]{:S(2)}) collective-permute-start(f32[128,256]{1,0:T(8,128)S(1)} %broadcast_select_fusion.refs_0_), channel_id=1, source_target_pairs={{0,24},{1,25},{2,26},{3,27},{4,28},{5,29},{6,30},{7,31},{8,0},{9,1... | collective-permute-start | bytes 393224 | tf_op jit(solution)/shard_map/errors_near/ppermute | solution.py:30
  59.4 9.4 %collective-permute-start.19 = (f32[128,256]{1,0:T(8,128)S(1)}, f32[128,256]{1,0:T(8,128)S(1)}, u32[]{:S(2)}, u32[]{:S(2)}) collective-permute-start(f32[128,256]{1,0:T(8,128)S(1)} %broadcast_select_fusion.refs_0_), channel_id=1, source_target_pairs={{0,8},{1,9},{2,10},{3,11},{4,12},{5,13},{6,14},{7,15},{8,16},{9,17... | collective-permute-start | bytes 393224 | tf_op jit(solution)/shard_map/errors_near/ppermute | solution.py:30
  61.4 7.4 %collective-permute-start.20 = (f32[128,256]{1,0:T(8,128)S(1)}, f32[128,256]{1,0:T(8,128)S(1)}, u32[]{:S(2)}, u32[]{:S(2)}) collective-permute-start(f32[128,256]{1,0:T(8,128)S(1)} %broadcast_select_fusion.refs_0_), channel_id=1, source_target_pairs={{0,16},{1,17},{2,18},{3,19},{4,20},{5,21},{6,22},{7,23},{8,24},{9,... | collective-permute-start | bytes 393224 | tf_op jit(solution)/shard_map/errors_near/ppermute | solution.py:30
  66.6 19.3 %collective-permute-start.24 = (f32[256,256]{1,0:T(8,128)S(1)}, f32[256,256]{1,0:T(8,128)S(1)}, u32[]{:S(2)}, u32[]{:S(2)}) collective-permute-start(f32[256,256]{1,0:T(8,128)S(1)} %pad_maximum_fusion.1), channel_id=1, source_target_pairs={{0,24},{1,25},{2,26},{3,27},{4,28},{5,29},{6,30},{7,31},{8,0},{9,1... | collective-permute-start | bytes 786440 | tf_op jit(solution)/shard_map/errors_far/ppermute | solution.py:30
  66.7 19.2 %collective-permute-start.22 = (f32[256,256]{1,0:T(8,128)S(1)}, f32[256,256]{1,0:T(8,128)S(1)}, u32[]{:S(2)}, u32[]{:S(2)}) collective-permute-start(f32[256,256]{1,0:T(8,128)S(1)} %pad_maximum_fusion.1), channel_id=1, source_target_pairs={{0,8},{1,9},{2,10},{3,11},{4,12},{5,13},{6,14},{7,15},{8,16},{9,17... | collective-permute-start | bytes 786440 | tf_op jit(solution)/shard_map/errors_far/ppermute | solution.py:30
  68.8 17.2 %collective-permute-start.27 = (f32[256,256]{1,0:T(8,128)S(1)}, f32[256,256]{1,0:T(8,128)S(1)}, u32[]{:S(2)}, u32[]{:S(2)}) collective-permute-start(f32[256,256]{1,0:T(8,128)S(1)} %pad_maximum_fusion.2), channel_id=1, source_target_pairs={{0,3},{1,0},{2,1},{3,2},{4,7},{5,4},{6,5},{7,6},{8,11},{9,8},{10,9... | collective-permute-start | bytes 786440 | tf_op jit(solution)/shard_map/errors_far/ppermute | solution.py:30
  72.1 13.9 %collective-permute-start.25 = (f32[256,256]{1,0:T(8,128)S(1)}, f32[256,256]{1,0:T(8,128)S(1)}, u32[]{:S(2)}, u32[]{:S(2)}) collective-permute-start(f32[256,256]{1,0:T(8,128)S(1)} %pad_maximum_fusion.2), channel_id=1, source_target_pairs={{0,1},{1,2},{2,3},{3,0},{4,5},{5,6},{6,7},{7,4},{8,9},{9,10},{10,1... | collective-permute-start | bytes 786440 | tf_op jit(solution)/shard_map/errors_far/ppermute | solution.py:30
  72.1 7.0 %collective-permute-start.26 = (f32[64,256]{1,0:T(8,128)S(1)}, f32[64,256]{1,0:T(8,128)S(1)}, u32[]{:S(2)}, u32[]{:S(2)}) collective-permute-start(f32[64,256]{1,0:T(8,128)S(1)} %slice.53), channel_id=1, source_target_pairs={{0,2},{1,3},{2,0},{3,1},{4,6},{5,7},{6,4},{7,5},{8,10},{9,11},{10,... | collective-permute-start | bytes 196616 | tf_op jit(solution)/shard_map/errors_far/ppermute | solution.py:30
  79.1 6.9 %collective-permute-start.23 = (f32[64,256]{1,0:T(8,128)S(1)}, f32[64,256]{1,0:T(8,128)S(1)}, u32[]{:S(2)}, u32[]{:S(2)}) collective-permute-start(f32[64,256]{1,0:T(8,128)S(1)} %slice.50), channel_id=1, source_target_pairs={{0,16},{1,17},{2,18},{3,19},{4,20},{5,21},{6,22},{7,23},{8,24},{9,... | collective-permute-start | bytes 196616 | tf_op jit(solution)/shard_map/errors_far/ppermute | solution.py:30
